TPU v7x, 128 devices: a whole 4x4x4 slice. The times are simulated.
128 devices in a mesh: dp: 8 (over z, y_hi), expert: 16 (over x, y_lo, core).
Axes of the slice: x: 4, y: 4 (y_hi: 2, y_lo: 2; y = y_hi * 2 + y_lo), z: 4, core: 2. Of those that a mesh axis runs over, the one named last changes fastest.
Arguments:
- tokens: bfloat16 [16384, 3072], P(('dp', 'expert')), may hold values from -64 to 64
- attn_param: bfloat16 [18432, 128], P('dp'), may hold values from -0.75 to 0.75
- expert_ids: int32 [16384, 1], P(('dp', 'expert')), may hold values from 0 to 15; in each aligned block of 128 rows (0 to 127, 128 to 255, ...) at most 10 rows name the same one
- gate_score: float32 [16384, 1], P(('dp', 'expert')), may hold values from 0.25 to 1
- w_in: bfloat16 [16, 3072, 2, 5376], P('expert', None, None, 'dp'), may hold values from -0.109375 to 0.109375
- w_out: bfloat16 [16, 5376, 3072], P('expert', 'dp'), may hold values from -0.078125 to 0.078125
- cotangent: bfloat16 [16384, 3072], P(('dp', 'expert')), may hold values from -24 to 24
Outputs:
- grad_tokens: bfloat16 [16384, 3072], P(('dp', 'expert'))
- attn_grad: float32 [18432, 128], P(('dp', 'expert'))
Inputs may be any that keep to these rules, and one draw needn't show every extreme that they name: `expert_ids`: each row names 1 different experts. In the rows of one device no expert is named more than 10 times, and in every draw some device's rows name some expert exactly 10 times.
All inputs are finite; a program needn't handle non-finite values.
Results may differ from a plain program's by a relative error of at most 0.02.
Values may be sent and summed in bfloat16 or wider, within the bound.
No kernel may reach another device: no remote copies, remote signals or barrier semaphores. Data moves between devices by JAX's collectives and lax.ppermute only.
A program may use at most 128 MiB of HBM per device.

v0:
```python
import jax
import jax.numpy as jnp
from jax import lax
from jax.sharding import PartitionSpec as P

EPSILON = 1e-05
MASKED = -1e30
PRECISE = lax.Precision.HIGHEST


def layer_norm(values):
    widened = values.astype(jnp.float32)
    center = widened - jnp.mean(widened, axis=-1, keepdims=True)
    inverse = lax.rsqrt(jnp.mean(center * center, axis=-1, keepdims=True) + EPSILON)
    return (center * inverse, inverse)


def norm_back(normed, inverse, upstream):
    mean_grad = jnp.mean(upstream, axis=-1, keepdims=True)
    mean_proj = jnp.mean(upstream * normed, axis=-1, keepdims=True)
    return inverse * (upstream - mean_grad - normed * mean_proj)


def slot_table(expert_ids, experts, capacity):
    flat_ids = expert_ids.reshape(-1)
    one_hot = (flat_ids[:, None] == jnp.arange(experts, dtype=jnp.int32)[None, :]).astype(jnp.int32)
    earlier = jnp.cumsum(one_hot, axis=0) - one_hot
    position = jnp.sum(earlier * one_hot, axis=1)
    target = flat_ids * capacity + position
    entries = flat_ids.shape[0]
    owners = (
        jnp.zeros((experts * capacity,), jnp.int32)
        .at[target]
        .set(jnp.arange(entries, dtype=jnp.int32))
    )
    filled = (
        jnp.zeros((experts * capacity,), jnp.int32).at[target].set(jnp.ones((entries,), jnp.int32))
    )
    return (owners, filled, target)


def contract(first_op, second_op, first_dim, second_dim):
    return lax.dot_general(
        first_op,
        second_op,
        (((first_dim,), (second_dim,)), ((), ())),
        preferred_element_type=jnp.float32,
    )


def per_device(tokens, attn_param, expert_ids, gate_score, w_in, w_out, cotangent):
    experts = lax.axis_size("expert")
    devices = lax.axis_size("dp") * experts
    seq_len, features = tokens.shape
    fanout = expert_ids.shape[1]
    head_dim = attn_param.shape[1]
    hidden_units = w_out.shape[1]
    capacity = seq_len * fanout * 5 // (4 * experts)
    score_scale = head_dim ** (-0.5)
    owners, filled, target = slot_table(expert_ids, experts, capacity)
    live_slot = (filled == 1)[:, None]
    source_rows = owners // fanout
    inner = w_in[0].reshape(features, 2 * hidden_units)
    outer = w_out[0]

    def pack_rows(rows):
        picked = jnp.take(rows, source_rows, axis=0)
        return jnp.where(live_slot, picked, jnp.zeros((), rows.dtype)).reshape(
            experts, capacity, features
        )

    cot_buffer = pack_rows(cotangent)
    packed = lax.all_gather(attn_param, "dp", axis=0, tiled=True)
    head_count = (packed.shape[0] // features - 2) // 2
    normed_one, inverse_one = layer_norm(tokens)
    normed_one_b = normed_one.astype(jnp.bfloat16)
    project = packed[: (head_count + 2) * features].reshape(head_count + 2, features, head_dim)
    out_blocks = packed[(head_count + 2) * features :].reshape(head_count, features, head_dim)
    projected = jnp.einsum(
        "td,jdc->tjc", normed_one_b, project, preferred_element_type=jnp.float32
    ).astype(jnp.bfloat16)
    queries = projected[:, :head_count]
    key_rows = projected[:, head_count]
    value_rows = projected[:, head_count + 1]
    scores = (
        jnp.einsum("qhc,kc->hqk", queries, key_rows, preferred_element_type=jnp.float32)
        * score_scale
    )
    causal = lax.broadcasted_iota(jnp.int32, (seq_len, seq_len), 0) >= lax.broadcasted_iota(
        jnp.int32, (seq_len, seq_len), 1
    )
    scores = jnp.where(causal[None], scores, MASKED)
    row_max = jnp.max(scores, axis=2, keepdims=True)
    raised = jnp.exp(scores - row_max)
    attention = raised / jnp.sum(raised, axis=2, keepdims=True)
    attention_b = attention.astype(jnp.bfloat16)
    context = jnp.einsum(
        "hqk,kc->qhc", attention_b, value_rows, preferred_element_type=jnp.float32
    ).astype(jnp.bfloat16)
    attn_out = jnp.einsum("thc,hdc->td", context, out_blocks, preferred_element_type=jnp.float32)
    residual = (tokens.astype(jnp.float32) + attn_out).astype(jnp.bfloat16)
    normed_two, inverse_two = layer_norm(residual)
    normed_buffer = pack_rows(normed_two.astype(jnp.bfloat16))
    normed_rows = lax.all_to_all(normed_buffer, "expert", split_axis=0, concat_axis=0, tiled=True)
    own_sources, slot_count, _ = normed_rows.shape
    all_normed = lax.all_gather(normed_rows, "dp", axis=0, tiled=True)
    all_cot = lax.all_gather(
        lax.all_to_all(cot_buffer, "expert", split_axis=0, concat_axis=0, tiled=True),
        "dp",
        axis=0,
        tiled=True,
    )
    row_count = own_sources * lax.axis_size("dp")
    inputs = all_normed
    inputs = inputs.reshape(row_count * slot_count, features)
    cot_part = all_cot
    cot_part = cot_part.reshape(row_count * slot_count, features)
    mixed_rows = jnp.dot(inputs, inner, preferred_element_type=jnp.float32)
    gate_part = mixed_rows[:, :hidden_units]
    up_part = mixed_rows[:, hidden_units:]
    squash = jax.nn.sigmoid(gate_part)
    grad_act = contract(cot_part, outer, 1, 1)
    grad_mixed = jnp.concatenate(
        [
            grad_act * up_part * squash * (1.0 + gate_part * (1.0 - squash)),
            grad_act * gate_part * squash,
        ],
        axis=1,
    ).astype(jnp.bfloat16)
    partial_rows = contract(grad_mixed, inner, 1, 1)
    summed = lax.psum_scatter(
        partial_rows.reshape(row_count, slot_count, features).astype(jnp.bfloat16),
        "dp",
        scatter_dimension=0,
        tiled=True,
    )
    arrived = lax.all_to_all(summed, "expert", split_axis=0, concat_axis=0, tiled=True)
    back_rows = jnp.take(arrived.reshape(experts * capacity, features), target, axis=0)
    back_rows = back_rows.reshape(seq_len, fanout, features)
    moe_grad = gate_score * back_rows[:, 0].astype(jnp.float32)
    grad_hidden = cotangent.astype(jnp.float32) + norm_back(normed_two, inverse_two, moe_grad)
    grad_hidden_b = grad_hidden.astype(jnp.bfloat16)
    grad_context = jnp.einsum(
        "td,hdc->thc", grad_hidden_b, out_blocks, preferred_element_type=jnp.float32
    )
    value_wide = value_rows.astype(jnp.float32)
    key_wide = key_rows.astype(jnp.float32)
    query_wide = queries.astype(jnp.float32)
    grad_attention = jnp.einsum("qhc,kc->hqk", grad_context, value_wide, precision=PRECISE)
    grad_value = jnp.einsum(
        "hqk,qhc->kc", attention_b.astype(jnp.float32), grad_context, precision=PRECISE
    )
    grad_scores = (
        attention
        * (grad_attention - jnp.sum(grad_attention * attention, axis=2, keepdims=True))
        * score_scale
    )
    grad_query = jnp.einsum("hqk,kc->qhc", grad_scores, key_wide, precision=PRECISE)
    grad_key = jnp.einsum("hqk,qhc->kc", grad_scores, query_wide, precision=PRECISE)
    grad_qkv = jnp.concatenate([grad_query, grad_key[:, None], grad_value[:, None]], axis=1).astype(
        jnp.bfloat16
    )
    grad_normed = jnp.einsum("tjc,jdc->td", grad_qkv, project, preferred_element_type=jnp.float32)
    grad_tokens = (grad_hidden + norm_back(normed_one, inverse_one, grad_normed)).astype(
        jnp.bfloat16
    )
    grad_project = jnp.einsum(
        "td,tjc->jdc", normed_one_b, grad_qkv, preferred_element_type=jnp.float32
    )
    grad_out = jnp.einsum("td,thc->hdc", grad_hidden_b, context, preferred_element_type=jnp.float32)
    grad_term = jnp.concatenate(
        [
            grad_project.reshape((head_count + 2) * features, head_dim),
            grad_out.reshape(head_count * features, head_dim),
        ],
        axis=0,
    )
    grad_term = grad_term * (seq_len * devices) ** (-0.5)
    attn_grad = lax.psum_scatter(grad_term, ("dp", "expert"), scatter_dimension=0, tiled=True)
    return (grad_tokens, attn_grad)


def solution(mesh):
    in_specs = (
        P(("dp", "expert"), None),
        P("dp", None),
        P(("dp", "expert"), None),
        P(("dp", "expert"), None),
        P("expert", None, None, "dp"),
        P("expert", "dp", None),
        P(("dp", "expert"), None),
    )
    out_specs = (P(("dp", "expert"), None), P(("dp", "expert"), None))
    return jax.shard_map(
        per_device, mesh=mesh, in_specs=in_specs, out_specs=out_specs, check_vma=False
    )
```

profile of v0, /device:TPU:0, one launch (start us, length us, event | category | flops | bytes accessed | tf_op | source)
XLA Modules:
  0.0 1274.2 jit_solution(12720174435123541563)
XLA Ops:
  12.4 2.2 gather_fusion.1
  15.2 73.6 %all-gather.4.cloned.1.call-done = bf16[18432,128]{1,0:T(8,128)(2,1)} async-done(((bf16[2304,128]{1,0:T(8,128)(2,1)}), bf16[18432,128]{1,0:T(8,128)(2,1)}) %all-gather.4.cloned.1.call-update) | async-done | bytes 4718608 | tf_op jit(solution)/shard_map/all_gather | solution.py:73
  99.8 2.7 select_select_fusion
  102.5 2.3 reshape.104
  104.8 26.5 %all_to_all.15 = bf16[16,10,3072]{2,1,0:T(8,128)(2,1)S(1)} all-to-all(bf16[16,10,3072]{2,1,0:T(8,128)(2,1)} %reshape.104), channel_id=1, replica_groups=mesh['dp'=8,'expert'=16] {'expert'}, dimensions={0} | all-to-all | bytes 1966080 | tf_op jit(solution)/shard_map/all_to_all | solution.py:104
  134.2 25.8 %all_to_all.16 = bf16[16,10,3072]{2,1,0:T(8,128)(2,1)S(1)} all-to-all(bf16[16,10,3072]{2,1,0:T(8,128)(2,1)} %reshape.102), channel_id=1, replica_groups=mesh['dp'=8,'expert'=16] {'expert'}, dimensions={0} | all-to-all | bytes 1966080 | tf_op jit(solution)/shard_map/all_to_all | solution.py:108
  161.8 84.7 %all-gather.8.cloned.1.call-done = bf16[128,10,3072]{2,0,1:T(8,128)(2,1)} async-done(((bf16[16,10,3072]{2,0,1:T(8,128)(2,1)}), bf16[128,10,3072]{2,0,1:T(8,128)(2,1)}) %all-gather.8.cloned.1.call-update) | async-done | bytes 7864336 | tf_op jit(solution)/shard_map/all_gather | solution.py:106
  246.5 12.2 copy.40
  258.7 13.7 %reshape.105 = bf16[1280,3072]{1,0:T(8,128)(2,1)} reshape(bf16[128,10,3072]{2,1,0:T(8,128)(2,1)} %copy.40) | data formatting | bytes 15728640 | tf_op jit(solution)/shard_map/reshape | solution.py:115
  272.4 76.7 %all-gather.6.cloned.1.call-done = bf16[128,10,3072]{2,0,1:T(8,128)(2,1)} async-done(((bf16[16,10,3072]{2,0,1:T(8,128)(2,1)}), bf16[128,10,3072]{2,0,1:T(8,128)(2,1)}) %all-gather.6.cloned.1.call-update) | async-done | bytes 7864336 | tf_op jit(solution)/shard_map/all_gather | solution.py:107
  349.1 12.1 copy.38
  361.2 13.7 %reshape.103 = bf16[1280,3072]{1,0:T(8,128)(2,1)} reshape(bf16[128,10,3072]{2,1,0:T(8,128)(2,1)} %copy.38) | data formatting | bytes 15728640 | tf_op jit(solution)/shard_map/reshape | solution.py:117
  374.9 14.4 %fusion.73 = f32[1280,1344]{0,1:T(8,128)S(1)} fusion(bf16[1280,3072]{1,0:T(8,128)(2,1)} %reshape.105, bf16[3072,1344]{0,1:T(8,128)(2,1)} %bitcast.132), kind=kOutput, calls=%fused_computation.117 | convolution fusion | flops 10569646080 | bytes 23003136 | tf_op jit(solution)/shard_map/dot_general | solution.py:118
  389.3 8.0 fusion.8
  397.3 3.7 copy.41
  401.1 5.0 concatenate.16
  406.1 4.7 copy.43
  410.8 3.7 copy.42
  414.5 5.0 concatenate.17
  419.5 4.7 copy.44
  424.2 17.9 %convolution_convert_fusion = bf16[128,10,3072]{2,0,1:T(8,128)(2,1)} fusion(bf16[3072,1344,1]{0,1,2:T(8,128)(2,1)} %bitcast.133, bf16[128,10,672]{0,2,1:T(8,128)(2,1)} %copy.44, bf16[128,10,672]{0,2,1:T(8,128)(2,1)} %copy.43), kind=kOutput, calls=%fused_computation.7 | convolution fusion | flops 10580459520 | bytes 19562496 | tf_op jit(solution)/shard_map/dot_general | solution.py:43
  442.1 109.4 %reduce-scatter.3.cloned.1.call-done = bf16[16,10,3072]{2,0,1:T(8,128)(2,1)} async-done(((bf16[128,10,3072]{2,0,1:T(8,128)(2,1)}), bf16[16,10,3072]{2,0,1:T(8,128)(2,1)}) %reduce-scatter.3.cloned.1.call-update) | async-done | bytes 983056 | tf_op jit(solution)/shard_map/reduce_scatter | solution.py:131
  551.5 3.0 copy.45
  554.5 4.4 all-to-all-start.2
  559.0 22.1 %all-to-all-done.2 = bf16[16,10,3072]{2,1,0:T(8,128)(2,1)} async-done(((bf16[16,10,3072]{2,1,0:T(8,128)(2,1)}), bf16[16,10,3072]{2,1,0:T(8,128)(2,1)}, u32[]{:S(2)}, u32[]{:S(2)}) %all-to-all-start.2) | async-done | bytes 983072 | tf_op jit(solution)/shard_map/all_to_all | solution.py:137
  590.1 2.3 convolution_bitcast_fusion.1
  592.3 3.7 convolution_bitcast_fusion
  596.1 6.6 copy.51
  602.6 3.6 copy.52
  606.2 9.4 maximum_multiply_fusion
  615.6 3.3 fusion.68
  620.5 647.3 %reduce-scatter.5.cloned.1.call-done = f32[144,128]{1,0:T(8,128)} async-done(((f32[18432,128]{1,0:T(8,128)}), f32[144,128]{1,0:T(8,128)}) %reduce-scatter.5.cloned.1.call-update) | async-done | bytes 73744 | tf_op jit(solution)/shard_map/reduce_scatter | solution.py:179
  (85 shorter events, 31.9 us)
Async XLA Ops:
  7.2 5.2 copy-start
  7.2 81.6 %all-gather.4.cloned.1.call-start = ((), (), s32[]{:S(2)}) async-start(), calls=%async_computation.5 | async-start | bytes 5308416 | tf_op jit(solution)/shard_map/all_gather | solution.py:73
  7.9 238.6 %all-gather.8.cloned.1.call-start = ((), (), s32[]{:S(2)}) async-start(), calls=%async_computation.7 | async-start | bytes 8847360 | tf_op jit(solution)/shard_map/all_gather | solution.py:106
  12.4 2.2 copy-start.1
  90.8 1.8 copy-start.7
  93.2 2.7 copy-start.13
  95.9 1.2 copy-start.5
  132.8 216.3 %all-gather.6.cloned.1.call-start = ((), (), s32[]{:S(2)}) async-start(), calls=%async_computation.6 | async-start | bytes 8847360 | tf_op jit(solution)/shard_map/all_gather | solution.py:107
  161.5 390.0 %reduce-scatter.3.cloned.1.call-start = ((), (), s32[]{:S(2)}) async-start(), calls=%async_computation.8 | async-start | bytes 8847360 | tf_op jit(solution)/shard_map/reduce_scatter | solution.py:131
  374.9 14.4 %copy-start.8 = (bf16[1280,3072]{1,0:T(8,128)(2,1)S(1)}, bf16[1280,3072]{1,0:T(8,128)(2,1)}, u32[]{:S(2)}) copy-start(bf16[1280,3072]{1,0:T(8,128)(2,1)} %reshape.103) | copy-start | bytes 23592964
  374.9 14.4 %copy-start.11 = (bf16[1,672,3072]{2,1,0:T(8,128)(2,1)S(1)}, bf16[1,672,3072]{2,1,0:T(8,128)(2,1)}, u32[]{:S(2)}) copy-start(bf16[1,672,3072]{2,1,0:T(8,128)(2,1)} %param.14) | copy-start | bytes 12386308
  554.5 26.6 %all-to-all-start.2 = ((bf16[16,10,3072]{2,1,0:T(8,128)(2,1)}), bf16[16,10,3072]{2,1,0:T(8,128)(2,1)}, u32[]{:S(2)}, u32[]{:S(2)}) async-start(bf16[16,10,3072]{2,1,0:T(8,128)(2,1)} %copy.45), calls=%async_computation.3 | async-start | bytes 3145728 | tf_op jit(solution)/shard_map/all_to_all | solution.py:137
  558.9 708.8 %reduce-scatter.5.cloned.1.call-start = ((), (), s32[]{:S(2)}) async-start(), calls=%async_computation.9 | async-start | bytes 9510912 | tf_op jit(solution)/shard_map/reduce_scatter | solution.py:179
  582.6 1.9 copy-start.10
  584.5 1.8 copy-start.9
  586.3 1.4 copy-start.6
  587.7 2.3 copy-start.3
  587.7 1.0 copy-start.12
  587.7 1.2 copy-start.14
  590.1 2.3 copy-start.2
  615.6 3.3 copy-start.4
Sparse Core Ops, SparseCore 0:
  10.3 78.4 all-gather.3
  132.9 113.4 all-gather.7
  248.8 100.2 all-gather.5
  442.2 109.2 reduce-scatter.2
  615.7 651.9 reduce-scatter.4
where the time goes:
time: 1280 us; the launch traced here: 1270 us
  waiting for transfers between devices  1010 us (79%)
  local copies, waits for them, and re-layouts  115 us (9%)
  matrix products  53.6 us (4%)
  blocking collectives  52.2 us (4%)
  other arithmetic  19.8 us (2%)
  between operations  14.1 us (1%)
    reduce_scatter x1, waiting for transfers between devices, per_device(): lax.psum_scatter(grad_term, ('dp', 'expert'), scatter_dimension=0, tiled=...  647 us
    reduce_scatter x1, waiting for transfers between devices, per_device(): lax.psum_scatter(partial_rows.reshape(row_count, slot_count, features).as...  109 us
    all_gather x1, waiting for transfers between devices, per_device(): all_normed = lax.all_gather(normed_rows, 'dp', axis=0, tiled=True)  84.7 us
    all_gather x1, waiting for transfers between devices, per_device(): lax.all_gather(lax.all_to_all(cot_buffer, 'expert', split_axis=0, concat_...  76.7 us
    all_gather x1, waiting for transfers between devices, per_device(): packed = lax.all_gather(attn_param, 'dp', axis=0, tiled=True)  73.6 us
    all_to_all x1, blocking collectives, per_device(): lax.all_to_all(normed_buffer, 'expert', split_axis=0, concat_axis=0, tile...  26.5 us
    dot_general x2, matrix products, contract(): lax.dot_general(first_op, second_op, (((first_dim,), (second_dim,)), ((),...  25.9 us
    all_to_all x1, blocking collectives, per_device(): lax.all_to_all(cot_buffer, 'expert', split_axis=0, concat_axis=0, tiled=T...  25.8 us
  transfers between devices with their start and end apart: 6, of which 6 were waited for; matrix products, arithmetic and copies ran while one was open for 3% of the time, Pallas kernels for 0%

commit v1 on v0

v1 whole, which is shorter than its diff:
```python
import jax
import jax.numpy as jnp
from jax import lax
from jax.sharding import Mesh, PartitionSpec as P

EPSILON = 1e-05
MASKED = -1e30
AXES = ("z", "yh", "x", "yl", "c")
DP = ("z", "yh")
EX = ("x", "yl", "c")
SIZES = (4, 2, 4, 2, 2)
EXPERTS = 16
N_DP = 8
CAP = 10
HEADS = 2
F32 = jnp.float32
BF16 = jnp.bfloat16


def layer_norm(values):
    widened = values.astype(F32)
    center = widened - jnp.mean(widened, axis=-1, keepdims=True)
    inverse = lax.rsqrt(jnp.mean(center * center, axis=-1, keepdims=True) + EPSILON)
    return (center * inverse, inverse)


def norm_back(normed, inverse, upstream):
    mean_grad = jnp.mean(upstream, axis=-1, keepdims=True)
    mean_proj = jnp.mean(upstream * normed, axis=-1, keepdims=True)
    return inverse * (upstream - mean_grad - normed * mean_proj)


def contract(first_op, second_op, first_dim, second_dim):
    return lax.dot_general(
        first_op,
        second_op,
        (((first_dim,), (second_dim,)), ((), ())),
        preferred_element_type=F32,
    )


def swap(values, axis):
    return lax.ppermute(values, axis, [(0, 1), (1, 0)])


def slot_matrix(expert_ids, seq_len):
    flat = expert_ids.reshape(-1)
    one_hot = (flat[:, None] == jnp.arange(EXPERTS, dtype=jnp.int32)[None, :]).astype(F32)
    rows = jnp.arange(seq_len)
    earlier = (rows[:, None] > rows[None, :]).astype(F32)
    before = jnp.dot(earlier, one_hot, preferred_element_type=F32)
    position = jnp.sum(before * one_hot, axis=1).astype(jnp.int32)
    target = flat * CAP + position
    return (jnp.arange(EXPERTS * CAP, dtype=jnp.int32)[:, None] == target[None, :]).astype(BF16)


def gather_params(attn_param):
    rows, head_dim = attn_param.shape
    half = rows // 2
    core = lax.axis_index("c")
    own = lax.dynamic_slice_in_dim(attn_param, core * half, half, 0)
    own = lax.all_to_all(
        jnp.broadcast_to(own[None], (N_DP, half, head_dim)), DP, split_axis=0, concat_axis=0, tiled=True
    )
    other = swap(own, "c")
    first = jnp.where(core == 0, own, other)
    second = jnp.where(core == 0, other, own)
    return jnp.stack([first, second], axis=1).reshape(N_DP * rows, head_dim)


def to_experts(buffer):
    features = buffer.shape[1]
    moved = lax.all_to_all(
        buffer.reshape(EXPERTS, CAP, features), EX, split_axis=0, concat_axis=0, tiled=True
    )
    return moved.reshape(EXPERTS * CAP, features)


def add_round(first, second):
    return (first.astype(F32) + second.astype(F32)).astype(BF16)


def scatter_grads(terms):
    head_dim = terms.shape[1]
    core = lax.axis_index("c")
    split = terms.astype(BF16).reshape(*SIZES, -1, head_dim)
    split = jnp.transpose(split, (4, 2, 3, 0, 1, 5, 6))
    split = split.reshape(2, 4, 2, N_DP, -1, head_dim)
    mine = lax.dynamic_index_in_dim(split, core, 0, keepdims=False)
    theirs = lax.dynamic_index_in_dim(split, 1 - core, 0, keepdims=False)
    summed = add_round(mine, swap(theirs, "c"))
    summed = summed.reshape(8, -1, head_dim)
    parts = lax.all_to_all(summed, ("x", "yl"), split_axis=0, concat_axis=0, tiled=True)
    summed = jnp.sum(parts.astype(F32), axis=0).astype(BF16).reshape(N_DP, -1, head_dim)
    parts = lax.all_to_all(summed, DP, split_axis=0, concat_axis=0, tiled=True)
    return jnp.sum(parts.astype(F32), axis=0)


def per_device(tokens, attn_param, expert_ids, gate_score, w_in, w_out, cotangent):
    seq_len, features = tokens.shape
    head_dim = attn_param.shape[1]
    hidden = w_out.shape[1]
    score_scale = head_dim ** (-0.5)
    devices = N_DP * EXPERTS
    slots = slot_matrix(expert_ids, seq_len)
    inner = jnp.transpose(w_in[0], (1, 2, 0))
    gate_map, up_map = inner[0], inner[1]
    outer = w_out[0]

    packed = gather_params(attn_param)
    cot_rows = to_experts(contract(slots, cotangent, 1, 0).astype(BF16))
    all_cot = lax.all_gather(cot_rows, DP, axis=0, tiled=True)

    normed_one, inverse_one = layer_norm(tokens)
    normed_one_b = normed_one.astype(BF16)
    blocks = packed.reshape(2 * HEADS + 2, features, head_dim)
    project = blocks[: HEADS + 2]
    out_blocks = blocks[HEADS + 2 :]
    projected = jnp.einsum(
        "td,jdc->tjc", normed_one_b, project, preferred_element_type=F32
    ).astype(BF16)
    queries = projected[:, :HEADS]
    key_rows = projected[:, HEADS]
    value_rows = projected[:, HEADS + 1]
    scores = jnp.einsum("qhc,kc->hqk", queries, key_rows, preferred_element_type=F32) * score_scale
    causal = lax.broadcasted_iota(jnp.int32, (seq_len, seq_len), 0) >= lax.broadcasted_iota(
        jnp.int32, (seq_len, seq_len), 1
    )
    scores = jnp.where(causal[None], scores, MASKED)
    row_max = jnp.max(scores, axis=2, keepdims=True)
    raised = jnp.exp(scores - row_max)
    attention = raised / jnp.sum(raised, axis=2, keepdims=True)
    attention_b = attention.astype(BF16)
    context = jnp.einsum(
        "hqk,kc->qhc", attention_b, value_rows, preferred_element_type=F32
    ).astype(BF16)
    attn_out = jnp.einsum("thc,hdc->td", context, out_blocks, preferred_element_type=F32)
    residual = (tokens.astype(F32) + attn_out).astype(BF16)
    normed_two, inverse_two = layer_norm(residual)
    normed_rows = to_experts(contract(slots, normed_two.astype(BF16), 1, 0).astype(BF16))
    all_normed = lax.all_gather(normed_rows, DP, axis=0, tiled=True)

    grad_act = contract(all_cot, outer, 1, 1)
    gate_part = contract(all_normed, gate_map, 1, 1)
    up_part = contract(all_normed, up_map, 1, 1)
    squash = jax.nn.sigmoid(gate_part)
    grad_gate = (grad_act * up_part * squash * (1.0 + gate_part * (1.0 - squash))).astype(BF16)
    grad_up = (grad_act * gate_part * squash).astype(BF16)
    partial_rows = (contract(grad_gate, gate_map, 1, 0) + contract(grad_up, up_map, 1, 0)).astype(BF16)
    summed = lax.psum_scatter(partial_rows, DP, scatter_dimension=0, tiled=True)
    arrived = to_experts(summed)
    back_rows = contract(slots, arrived, 0, 0)
    moe_grad = gate_score * back_rows
    grad_hidden = cotangent.astype(F32) + norm_back(normed_two, inverse_two, moe_grad)
    grad_hidden_b = grad_hidden.astype(BF16)
    grad_context = jnp.einsum(
        "td,hdc->thc", grad_hidden_b, out_blocks, preferred_element_type=F32
    )
    grad_context_b = grad_context.astype(BF16)
    grad_attention = jnp.einsum(
        "qhc,kc->hqk", grad_context_b, value_rows, preferred_element_type=F32
    )
    grad_value = jnp.einsum("hqk,qhc->kc", attention_b, grad_context_b, preferred_element_type=F32)
    grad_scores = (
        attention
        * (grad_attention - jnp.sum(grad_attention * attention, axis=2, keepdims=True))
        * score_scale
    )
    grad_scores_b = grad_scores.astype(BF16)
    grad_query = jnp.einsum("hqk,kc->qhc", grad_scores_b, key_rows, preferred_element_type=F32)
    grad_key = jnp.einsum("hqk,qhc->kc", grad_scores_b, queries, preferred_element_type=F32)
    grad_qkv = jnp.concatenate([grad_query, grad_key[:, None], grad_value[:, None]], axis=1).astype(BF16)
    grad_project = jnp.einsum("td,tjc->jdc", normed_one_b, grad_qkv, preferred_element_type=F32)
    grad_out = jnp.einsum("td,thc->hdc", grad_hidden_b, context, preferred_element_type=F32)
    grad_term = jnp.concatenate(
        [grad_project.reshape(-1, head_dim), grad_out.reshape(-1, head_dim)], axis=0
    )
    attn_grad = scatter_grads(grad_term * (seq_len * devices) ** (-0.5))
    grad_normed = jnp.einsum("tjc,jdc->td", grad_qkv, project, preferred_element_type=F32)
    grad_tokens = (grad_hidden + norm_back(normed_one, inverse_one, grad_normed)).astype(BF16)
    return (grad_tokens, attn_grad)


def solution(mesh):
    fine = Mesh(mesh.devices.reshape(SIZES), AXES)
    rows = P(AXES, None)
    in_specs = (
        rows,
        P(DP, None),
        rows,
        rows,
        P(EX, None, None, DP),
        P(EX, DP, None),
        rows,
    )
    return jax.shard_map(
        per_device, mesh=fine, in_specs=in_specs, out_specs=(rows, rows), check_vma=False
    )
```

time: 1280 us -> 587 us (0.46)
  waiting for transfers between devices: 1010 us -> 308 us
  local copies, waits for them, and re-layouts: 115 us -> 31 us
  blocking collectives: 52.2 us -> 105 us
  matrix products: 53.6 us -> 93.1 us
    reduce_scatter x2 -> x1, waiting for transfers between devices: 757 us -> 109 us  [per_device(): summed = lax.psum_scatter(partial_rows, DP, scatter_dimension=0, tiled=True)]
    all_gather x3 -> x2, waiting for transfers between devices: 235 us -> 130 us  [the longest x1 91.8 us: per_device(): all_normed = lax.all_gather(normed_rows, DP, axis=0, tiled=True)]
    all_to_all x2 -> x3, blocking collectives: 52.2 us -> 105 us  [the longest x2 55.8 us: to_experts(): lax.all_to_all(buffer.reshape(EXPERTS, CAP, features), EX, split_axis=0,...]
    dot_general x2 -> x7, matrix products: 25.9 us -> 76.2 us  [contract(): lax.dot_general(first_op, second_op, (((first_dim,), (second_dim,)), ((),...]
    all_to_all x1 -> x3, waiting for transfers between devices: 22.1 us -> 59.5 us  [the longest x1 31.3 us: scatter_grads(): lax.all_to_all(summed, ('x', 'yl'), split_axis=0, concat_axis=0, tiled=True)]
    all_gather x2 -> x0, local copies, waits for them, and re-layouts: 24.3 us -> none  [the longest x1 12.2 us: per_device(): all_normed = lax.all_gather(normed_rows, 'dp', axis=0, tiled=True)]
    reshape x5 -> x6, local copies, waits for them, and re-layouts: 32.6 us -> 13.2 us  [the longest x3 7.08 us: to_experts(): return moved.reshape(EXPERTS * CAP, features)]
    concatenate x4 -> x0, local copies, waits for them, and re-layouts: 19.4 us -> none  [per_device(): jnp.concatenate([grad_act * up_part * squash * (1.0 + gate_part * (1.0 -...]
  transfers between devices with their start and end apart: 6 -> 8, of which waited for: 6 -> 8; matrix products, arithmetic and copies ran while one was open for 3% -> 5% of each run, Pallas kernels for 0% -> 0%
where the time goes in v1:
time: 587 us; the launch traced here: 586 us
  waiting for transfers between devices  308 us (52%)
  blocking collectives  105 us (18%)
  matrix products  93.1 us (16%)
  local copies, waits for them, and re-layouts  31 us (5%)
  other arithmetic  21.8 us (4%)
  between operations  14 us (2%)
  starting transfers between devices  13.3 us (2%)
    reduce_scatter x1, waiting for transfers between devices, per_device(): summed = lax.psum_scatter(partial_rows, DP, scatter_dimension=0, tiled=True)  109 us
    all_gather x1, waiting for transfers between devices, per_device(): all_normed = lax.all_gather(normed_rows, DP, axis=0, tiled=True)  91.8 us
    dot_general x7, matrix products, contract(): lax.dot_general(first_op, second_op, (((first_dim,), (second_dim,)), ((),...  76.2 us
    all_to_all x2, blocking collectives, to_experts(): lax.all_to_all(buffer.reshape(EXPERTS, CAP, features), EX, split_axis=0,...  55.8 us
    all_to_all x1, blocking collectives, gather_params(): lax.all_to_all(jnp.broadcast_to(own[None], (N_DP, half, head_dim)), DP, s...  48.9 us
    all_gather x1, waiting for transfers between devices, per_device(): all_cot = lax.all_gather(cot_rows, DP, axis=0, tiled=True)  38.6 us
    all_to_all x1, waiting for transfers between devices, scatter_grads(): lax.all_to_all(summed, ('x', 'yl'), split_axis=0, concat_axis=0, tiled=True)  31.3 us
    all_to_all x1, waiting for transfers between devices, to_experts(): lax.all_to_all(buffer.reshape(EXPERTS, CAP, features), EX, split_axis=0,...  22.2 us
  transfers between devices with their start and end apart: 8, of which 8 were waited for; matrix products, arithmetic and copies ran while one was open for 5% of the time, Pallas kernels for 0%

profile of v1, /device:TPU:0, one launch (start us, length us, event | category | flops | bytes accessed | tf_op | source)
XLA Modules:
  0.0 586.2 jit_solution(5601503638935949639)
XLA Ops:
  8.8 2.5 convolution_convert_fusion.1
  12.7 27.5 %all_to_all.30 = bf16[16,10,3072]{2,1,0:T(8,128)(2,1)} all-to-all(bf16[16,10,3072]{2,1,0:T(8,128)(2,1)S(1)} %reshape.108), channel_id=1, replica_groups=mesh['z'=4,'yh'=2,'x'=4,'yl'=2,'c'=2] {'x','yl','c'}, dimensions={0} | all-to-all | bytes 1966080 | tf_op jit(solution)/shard_map/all_to_all | solution.py:73
  40.2 2.4 reshape.109
  43.0 48.9 %all_to_all.31 = bf16[8,1152,128]{2,1,0:T(8,128)(2,1)} all-to-all(bf16[8,1152,128]{2,1,0:T(8,128)(2,1)S(1)} %broadcast_in_dim.20), channel_id=1, replica_groups=mesh['z'=4,'yh'=2,'x'=4,'yl'=2,'c'=2] {'z','yh'}, dimensions={0} | all-to-all | bytes 4718592 | tf_op jit(solution)/shard_map/all_to_all | solution.py:62
  92.4 4.3 collective-permute-done
  96.7 2.7 select_bitcast_fusion.1
  107.2 2.4 reshape.110
  109.6 28.3 %all_to_all.32 = bf16[16,10,3072]{2,1,0:T(8,128)(2,1)} all-to-all(bf16[16,10,3072]{2,1,0:T(8,128)(2,1)} %reshape.110), channel_id=1, replica_groups=mesh['z'=4,'yh'=2,'x'=4,'yl'=2,'c'=2] {'x','yl','c'}, dimensions={0} | all-to-all | bytes 1966080 | tf_op jit(solution)/shard_map/all_to_all | solution.py:73
  137.9 2.4 reshape.111
  140.3 38.6 %all-gather.3.cloned.1.call-done = bf16[1280,3072]{1,0:T(8,128)(2,1)} async-done(((bf16[160,3072]{1,0:T(8,128)(2,1)}), bf16[1280,3072]{1,0:T(8,128)(2,1)}) %all-gather.3.cloned.1.call-update) | async-done | bytes 7864336 | tf_op jit(solution)/shard_map/all_gather | solution.py:112
  179.0 10.8 %fusion.4 = f32[1280,672]{0,1:T(8,128)} fusion(bf16[1280,3072]{1,0:T(8,128)(2,1)} %all-gather.3.cloned.1.call-done, bf16[1,672,3072]{2,1,0:T(8,128)(2,1)} %param.12), kind=kOutput, calls=%fused_computation.11 | convolution fusion | flops 5284823040 | bytes 15433728 | tf_op jit(solution)/shard_map/dot_general | solution.py:34
  189.8 91.8 %all-gather.5.cloned.1.call-done = bf16[1280,3072]{1,0:T(8,128)(2,1)} async-done(((bf16[160,3072]{1,0:T(8,128)(2,1)}), bf16[1280,3072]{1,0:T(8,128)(2,1)}) %all-gather.5.cloned.1.call-update) | async-done | bytes 7864336 | tf_op jit(solution)/shard_map/all_gather | solution.py:141
  281.6 10.8 %fusion.9 = f32[1280,672]{0,1:T(8,128)} fusion(bf16[1280,3072]{1,0:T(8,128)(2,1)} %all-gather.5.cloned.1.call-done, bf16[2,672,3072]{2,1,0:T(8,128)(2,1)} %bitcast.136), kind=kOutput, calls=%fused_computation.23 | convolution fusion | flops 5284823040 | bytes 15433728 | tf_op jit(solution)/shard_map/dot_general | solution.py:34
  292.4 34.2 %fusion.8 = f32[1280,3072]{1,0:T(8,128)} fusion(bf16[2,672,3072]{2,1,0:T(8,128)(2,1)} %bitcast.137, f32[1280,672]{0,1:T(8,128)} %fusion.9, f32[1280,672]{0,1:T(8,128)} %fusion.4, bf16[1280,3072]{1,0:T(8,128)(2,1)} %all-gather.5.cloned.1.call-done), kind=kOutput, calls=%fused_computation.22 | convolution fusion | flops 10578247680 | bytes 38731776 | tf_op jit(solution)/shard_map/dot_general | solution.py:34
  326.5 14.5 %add_convert_fusion = bf16[1280,3072]{1,0:T(8,128)(2,1)} fusion(f32[1280,3072]{1,0:T(8,128)} %fusion.8, bf16[2,672,3072]{2,1,0:T(8,128)(2,1)} %bitcast.138, f32[1280,672]{0,1:T(8,128)} %fusion.4, f32[1280,672]{0,1:T(8,128)} %fusion.9), kind=kOutput, calls=%fused_computation.2 | convolution fusion | flops 5297848320 | bytes 34603008 | tf_op jit(solution)/shard_map/dot_general | solution.py:34
  341.1 109.2 %reduce-scatter.2.cloned.1.call-done = bf16[160,3072]{1,0:T(8,128)(2,1)} async-done(((bf16[1280,3072]{1,0:T(8,128)(2,1)}), bf16[160,3072]{1,0:T(8,128)(2,1)}) %reduce-scatter.2.cloned.1.call-update) | async-done | bytes 983056 | tf_op jit(solution)/shard_map/reduce_scatter | solution.py:150
  450.3 2.3 reshape.112
  452.7 4.6 all-to-all-start.3
  457.2 22.2 %all-to-all-done.3 = bf16[16,10,3072]{2,1,0:T(8,128)(2,1)} async-done(((bf16[16,10,3072]{2,1,0:T(8,128)(2,1)}), bf16[16,10,3072]{2,1,0:T(8,128)(2,1)}, u32[]{:S(2)}, u32[]{:S(2)}) %all-to-all-start.3) | async-done | bytes 983072 | tf_op jit(solution)/shard_map/all_to_all | solution.py:73
  490.9 3.7 convolution_bitcast_fusion
  494.7 6.6 %copy.39 = f32[4,3072,128]{2,1,0:T(8,128)} copy(f32[4,3072,128]{1,2,0:T(8,128)} %convolution_bitcast_fusion) | data formatting | bytes 12582912 | tf_op jit(solution)/shard_map/td,tjc->jdc/transpose | solution.py:173
  501.3 3.6 copy.40
  504.8 5.6 fusion.2
  513.8 4.9 collective-permute-done.1
  518.7 4.4 fusion.3
  523.1 4.4 all-to-all-start.4
  527.5 4.2 fusion.94
  531.7 31.3 %all-to-all-done.4 = bf16[8,1152,128]{2,1,0:T(8,128)(2,1)} async-done(((bf16[8,1152,128]{2,1,0:T(8,128)(2,1)}), bf16[8,1152,128]{2,1,0:T(8,128)(2,1)}, u32[]{:S(2)}, u32[]{:S(2)}) %all-to-all-start.4) | async-done | bytes 2359328 | tf_op jit(solution)/shard_map/all_to_all | solution.py:93
  563.0 2.8 reduce_sum.131
  565.8 4.2 all-to-all-start.5
  570.0 2.9 fusion.28
  573.0 6.0 %all-to-all-done.5 = bf16[8,144,128]{2,1,0:T(8,128)(2,1)S(1)} async-done(((bf16[8,144,128]{2,1,0:T(8,128)(2,1)}), bf16[8,144,128]{2,1,0:T(8,128)(2,1)S(1)}, u32[]{:S(2)}, u32[]{:S(2)}) %all-to-all-start.5) | async-done | bytes 294944 | tf_op jit(solution)/shard_map/all_to_all | solution.py:95
  (60 shorter events, 27.2 us)
Async XLA Ops:
  7.2 35.5 %copy-start = (bf16[2304,128]{1,0:T(8,128)(2,1)S(1)}, bf16[2304,128]{1,0:T(8,128)(2,1)}, u32[]{:S(2)}) copy-start(bf16[2304,128]{1,0:T(8,128)(2,1)} %param.8) | copy-start | bytes 1769476
  7.2 171.8 %all-gather.3.cloned.1.call-start = ((), (), s32[]{:S(2)}) async-start(), calls=%async_computation.7 | async-start | bytes 8847360 | tf_op jit(solution)/shard_map/all_gather | solution.py:112
  42.6 239.0 %all-gather.5.cloned.1.call-start = ((), (), s32[]{:S(2)}) async-start(), calls=%async_computation.8 | async-start | bytes 8847360 | tf_op jit(solution)/shard_map/all_gather | solution.py:141
  43.0 48.9 %copy-start.4 = (bf16[128,3072]{1,0:T(8,128)(2,1)S(1)}, bf16[128,3072]{1,0:T(8,128)(2,1)}, u32[]{:S(2)}) copy-start(bf16[128,3072]{1,0:T(8,128)(2,1)} %param.7) | copy-start | bytes 2359300
  91.8 4.9 collective-permute-start
  99.9 2.3 copy-start.6
  140.3 310.0 %reduce-scatter.2.cloned.1.call-start = ((), (), s32[]{:S(2)}) async-start(), calls=%async_computation.9 | async-start | bytes 8847360 | tf_op jit(solution)/shard_map/reduce_scatter | solution.py:150
  452.7 29.1 %copy-start.8 = (f32[128,1]{0,1:T(1,128)S(1)}, f32[128,1]{0,1:T(1,128)}, u32[]{:S(2)}) copy-start(f32[128,1]{0,1:T(1,128)} %param.10) | copy-start | bytes 1540
  452.7 26.7 %all-to-all-start.3 = ((bf16[16,10,3072]{2,1,0:T(8,128)(2,1)}), bf16[16,10,3072]{2,1,0:T(8,128)(2,1)}, u32[]{:S(2)}, u32[]{:S(2)}) async-start(bf16[16,10,3072]{2,1,0:T(8,128)(2,1)} %reshape.112), calls=%async_computation.4 | async-start | bytes 3145728 | tf_op jit(solution)/shard_map/all_to_all | solution.py:73
  481.7 1.9 copy-start.7
  484.3 1.2 copy-start.2
  487.3 1.4 copy-start.3
  511.0 2.8 copy-start.5
  513.8 4.9 collective-permute-start.1
  523.1 39.9 %all-to-all-start.4 = ((bf16[8,1152,128]{2,1,0:T(8,128)(2,1)}), bf16[8,1152,128]{2,1,0:T(8,128)(2,1)}, u32[]{:S(2)}, u32[]{:S(2)}) async-start(bf16[8,1152,128]{2,1,0:T(8,128)(2,1)} %bitcast.134), calls=%async_computation.5 | async-start | bytes 4718592 | tf_op jit(solution)/shard_map/all_to_all | solution.py:93
  565.8 13.2 %all-to-all-start.5 = ((bf16[8,144,128]{2,1,0:T(8,128)(2,1)}), bf16[8,144,128]{2,1,0:T(8,128)(2,1)S(1)}, u32[]{:S(2)}, u32[]{:S(2)}) async-start(bf16[8,144,128]{2,1,0:T(8,128)(2,1)} %bitcast.40), calls=%async_computation.6 | async-start | bytes 589824 | tf_op jit(solution)/shard_map/all_to_all | solution.py:95
  570.0 9.6 %copy-start.1 = (bf16[2304,128]{1,0:T(8,128)(2,1)S(1)}, bf16[2304,128]{1,0:T(8,128)(2,1)}, u32[]{:S(2)}) copy-start(bf16[2304,128]{1,0:T(8,128)(2,1)} %param.8) | copy-start | bytes 1769476
Sparse Core Ops, SparseCore 0:
  42.7 136.2 all-gather.2
  181.3 100.2 all-gather.4
  341.2 109.0 reduce-scatter.1

commit v2 on v1

v2 whole, which is shorter than its diff:
```python
import jax
import jax.numpy as jnp
from jax import lax
from jax.experimental import pallas as pl
from jax.experimental.pallas import tpu as pltpu
from jax.sharding import Mesh, PartitionSpec as P

EPSILON = 1e-05
MASKED = -1e30
AXES = ("z", "yh", "x", "yl", "c")
DP = ("z", "yh")
EX = ("x", "yl", "c")
CHIPS = ("z", "yh", "x", "yl")
SIZES = (4, 2, 4, 2, 2)
EXPERTS = 16
N_DP = 8
CAP = 10
MAIN = 8
HEADS = 2
HALF = 80
PADDED = 768
F32 = jnp.float32
BF16 = jnp.bfloat16


def layer_norm(values):
    widened = values.astype(F32)
    center = widened - jnp.mean(widened, axis=-1, keepdims=True)
    inverse = lax.rsqrt(jnp.mean(center * center, axis=-1, keepdims=True) + EPSILON)
    return (center * inverse, inverse)


def norm_back(normed, inverse, upstream):
    mean_grad = jnp.mean(upstream, axis=-1, keepdims=True)
    mean_proj = jnp.mean(upstream * normed, axis=-1, keepdims=True)
    return inverse * (upstream - mean_grad - normed * mean_proj)


def contract(first_op, second_op, first_dim, second_dim):
    return lax.dot_general(
        first_op,
        second_op,
        (((first_dim,), (second_dim,)), ((), ())),
        preferred_element_type=F32,
    )


def swap(values, axis):
    return lax.ppermute(values, axis, [(0, 1), (1, 0)])


def along_z(values, shift):
    return lax.ppermute(values, "z", [(i, (i + shift) % 4) for i in range(4)])


def exchange(blocks, axes):
    return lax.all_to_all(blocks, axes, split_axis=0, concat_axis=0, tiled=True)


def after(value, *earlier):
    return lax.optimization_barrier((value,) + earlier)[0]


def add_round(first, *others):
    total = first.astype(F32)
    for other in others:
        total = total + other.astype(F32)
    return total.astype(BF16)


def slot_matrix(expert_ids, seq_len):
    flat = expert_ids.reshape(-1)
    one_hot = (flat[:, None] == jnp.arange(EXPERTS, dtype=jnp.int32)[None, :]).astype(F32)
    rows = jnp.arange(seq_len)
    earlier = (rows[:, None] > rows[None, :]).astype(F32)
    before = jnp.dot(earlier, one_hot, preferred_element_type=F32)
    position = jnp.sum(before * one_hot, axis=1).astype(jnp.int32)
    rest = CAP - MAIN
    target = jnp.where(
        position < MAIN, flat * MAIN + position, EXPERTS * MAIN + flat * rest + position - MAIN
    )
    return (jnp.arange(EXPERTS * CAP, dtype=jnp.int32)[:, None] == target[None, :]).astype(BF16)


def gather_params(attn_param):
    rows, head_dim = attn_param.shape
    half = rows // 2
    core = lax.axis_index("c")
    own = lax.dynamic_slice_in_dim(attn_param, core * half, half, 0)
    own = exchange(jnp.broadcast_to(own[None], (N_DP, half, head_dim)), DP)
    other = swap(own, "c")
    first = jnp.where(core == 0, own, other)
    second = jnp.where(core == 0, other, own)
    return jnp.stack([first, second], axis=1).reshape(N_DP * rows, head_dim)


def between_experts(rows):
    features = rows.shape[1]
    cut = EXPERTS * MAIN
    extra = rows[cut:].reshape(cut, -1)
    packed = jnp.concatenate([rows[:cut], extra], axis=1)
    width = packed.shape[1]
    packed = exchange(packed.reshape(EXPERTS, MAIN, width), EX).reshape(cut, width)
    extra = packed[:, features:].reshape(-1, features)
    return packed[:, :features], extra


def spread(main, extra):
    one = main[:HALF]
    two = jnp.concatenate([main[HALF:], extra], axis=0)
    one_z = {0: one, 1: along_z(one, 1), 3: along_z(one, -1), 2: along_z(one, 2)}
    two_y = swap(two, "yh")
    one_y = {0: swap(one, "yh")}
    for s in (1, 3, 2):
        one_y[s] = swap(one_z[s], "yh")
    late, late_y = after(two, one_z[1], one_z[3]), after(two_y, one_z[1], one_z[3])
    two_z, two_yz = {0: two}, {0: two_y}
    for s in (1, 3, 2):
        two_z[s] = along_z(late, s)
    for s in (1, 3, 2):
        two_yz[s] = along_z(late_y, s)
    return (one_z, one_y), (two_z, two_yz)


def collect(first, second):
    early = [along_z(first[0][s], -s) for s in (1, 3, 2)]
    early_y = swap(second[1][0], "yh")
    late = [along_z(first[1][s], -s) for s in (1, 3, 2)]
    swapped = {s: swap(second[1][s], "yh") for s in (1, 3, 2)}
    far = add_round(first[1][0], *late)
    far = swap(far, "yh")
    back = [along_z(add_round(second[0][s], swapped[s]), -s) for s in (1, 3, 2)]
    one = add_round(first[0][0], far, *early)
    two = add_round(second[0][0], early_y, *back)
    return one, two


def expert_kernel(count, rows, tall, *refs):
    normed_refs, cot_refs = refs[:count], refs[count : 2 * count]
    inner_ref, outer_ref = refs[2 * count : 2 * count + 2]
    out_refs = refs[2 * count + 2 : 3 * count + 2]
    (normed, cot, gate_map, up_map, outer_map, grad_gate, grad_up, result, row_sem, map_sem, out_sem) = refs[
        3 * count + 2 :
    ]
    hidden, features = outer_ref.shape

    def load(source, target, sem):
        copy = pltpu.make_async_copy(source, target, sem)
        copy.start()
        return copy

    pieces = [(0, 256), (256, 256), (512, hidden - 512)]
    rows_in = [load(ref, normed.at[pl.ds(i * rows, rows)], row_sem.at[0, i]) for i, ref in enumerate(normed_refs)]
    maps_in = []
    for i, (start, size) in enumerate(pieces):
        at = pl.ds(start, size)
        maps_in.append(
            [
                load(inner_ref.at[0, at], gate_map.at[at], map_sem.at[0, i]),
                load(inner_ref.at[1, at], up_map.at[at], map_sem.at[1, i]),
                load(outer_ref.at[at], outer_map.at[at], map_sem.at[2, i]),
            ]
        )
        if i == 0:
            rows_in += [
                load(ref, cot.at[pl.ds(j * rows, rows)], row_sem.at[1, j]) for j, ref in enumerate(cot_refs)
            ]
    blank = jnp.zeros((PADDED - hidden, features), BF16)
    for ref in (gate_map, up_map, outer_map):
        ref[pl.ds(hidden, PADDED - hidden)] = blank
    for copy in rows_in:
        copy.wait()
    steps = count * rows // tall

    for i in range(len(pieces)):
        for copy in maps_in[i]:
            copy.wait()
        at = pl.ds(i * 256, 256)

        @pl.loop(0, steps)
        def _(step):
            here = pl.ds(pl.multiple_of(step * tall, 16), tall)
            gate_part = contract(normed[here], gate_map[at], 1, 1)
            up_part = contract(normed[here], up_map[at], 1, 1)
            grad_act = contract(cot[here], outer_map[at], 1, 1)
            squash = 1.0 / (1.0 + jnp.exp(-gate_part))
            scaled = grad_act * squash
            grad_gate[here, at] = (scaled * up_part * (1.0 + gate_part * (1.0 - squash))).astype(BF16)
            grad_up[here, at] = (scaled * gate_part).astype(BF16)

    wide = 512
    copies = []
    for n in range(features // wide):
        lanes = pl.ds(n * wide, wide)

        @pl.loop(0, steps)
        def _(step):
            here = pl.ds(pl.multiple_of(step * tall, 16), tall)
            result[here, lanes] = (
                contract(grad_gate[here], gate_map[:, lanes], 1, 0)
                + contract(grad_up[here], up_map[:, lanes], 1, 0)
            ).astype(BF16)

        copies += [
            load(result.at[pl.ds(i * rows, rows), lanes], ref.at[:, lanes], out_sem.at[n, i])
            for i, ref in enumerate(out_refs)
        ]
    for copy in copies:
        copy.wait()


def experts(normed_blocks, cot_blocks, inner, outer, tall):
    count = len(normed_blocks)
    rows, features = normed_blocks[0].shape
    hidden = outer.shape[0]
    total = count * rows
    anywhere = pl.BlockSpec(memory_space=pl.ANY)
    return pl.pallas_call(
        lambda *refs: expert_kernel(count, rows, tall, *refs),
        out_shape=[jax.ShapeDtypeStruct((rows, features), BF16)] * count,
        in_specs=[anywhere] * (2 * count + 2),
        out_specs=[anywhere] * count,
        scratch_shapes=[
            pltpu.VMEM((total, features), BF16),
            pltpu.VMEM((total, features), BF16),
            pltpu.VMEM((PADDED, features), BF16),
            pltpu.VMEM((PADDED, features), BF16),
            pltpu.VMEM((PADDED, features), BF16),
            pltpu.VMEM((total, PADDED), BF16),
            pltpu.VMEM((total, PADDED), BF16),
            pltpu.VMEM((total, features), BF16),
            pltpu.SemaphoreType.DMA((2, count)),
            pltpu.SemaphoreType.DMA((3, 3)),
            pltpu.SemaphoreType.DMA((features // 512, count)),
        ],
        compiler_params=pltpu.CompilerParams(vmem_limit_bytes=48 * 1024 * 1024),
        cost_estimate=pl.CostEstimate(
            flops=10 * total * features * hidden,
            bytes_accessed=6 * total * features + 6 * hidden * features,
            transcendentals=total * hidden,
        ),
    )(*normed_blocks, *cot_blocks, inner, outer)


def param_kernel(scale, head_dim, core_ref, normed_ref, hidden_ref, grads_ref, context_ref, out_ref, terms):
    features = normed_ref.shape[1]
    tile = 1024
    for block in range(6):
        left_ref = normed_ref if block < 4 else hidden_ref
        right = (grads_ref[:, block * head_dim : (block + 1) * head_dim] if block < 4
                 else context_ref[:, (block - 4) * head_dim : (block - 3) * head_dim])
        for start in range(0, features, tile):
            part = contract(left_ref[:, start : start + tile], right, 0, 0) * scale
            terms[pl.ds(block * features + start, tile)] = part.astype(BF16)
    core = core_ref[0]

    @pl.loop(0, out_ref.shape[0])
    def _(group):
        size = out_ref.shape[1]
        out_ref[group] = terms[pl.ds(pl.multiple_of((2 * group + core) * size, 16), size)]


def param_terms(core, normed, hidden, grads, context, scale, head_dim):
    features = normed.shape[1]
    rows = 6 * features
    whole = pl.BlockSpec(memory_space=pltpu.VMEM)
    return pl.pallas_call(
        lambda *refs: param_kernel(scale, head_dim, *refs),
        out_shape=jax.ShapeDtypeStruct((64, rows // 128, head_dim), BF16),
        in_specs=[pl.BlockSpec(memory_space=pltpu.SMEM)] + [whole] * 4,
        out_specs=whole,
        scratch_shapes=[pltpu.VMEM((rows, head_dim), BF16)],
        compiler_params=pltpu.CompilerParams(vmem_limit_bytes=40 * 1024 * 1024),
        cost_estimate=pl.CostEstimate(
            flops=2 * rows * head_dim * normed.shape[0], bytes_accessed=8 * 1024 * 1024, transcendentals=0
        ),
    )(core, normed, hidden, grads, context)


def per_device(tokens, attn_param, expert_ids, gate_score, w_in, w_out, cotangent):
    seq_len, features = tokens.shape
    head_dim = attn_param.shape[1]
    score_scale = head_dim ** (-0.5)
    devices = N_DP * EXPERTS
    slots = slot_matrix(expert_ids, seq_len)
    inner = jnp.transpose(w_in[0], (1, 2, 0))
    outer = w_out[0]

    packed = gather_params(attn_param)
    cot_main, cot_extra = between_experts(contract(slots, cotangent, 1, 0).astype(BF16))
    cot_one, cot_two = spread(cot_main, cot_extra)

    normed_one, inverse_one = layer_norm(tokens)
    normed_one_b = normed_one.astype(BF16)
    normed_both = jnp.concatenate([normed_one_b, swap(normed_one_b, "c")], axis=0)
    blocks = packed.reshape(2 * HEADS + 2, features, head_dim)
    project = blocks[: HEADS + 2]
    out_blocks = blocks[HEADS + 2 :]
    projected = jnp.einsum(
        "td,jdc->tjc", normed_one_b, project, preferred_element_type=F32
    ).astype(BF16)
    queries = projected[:, :HEADS]
    key_rows = projected[:, HEADS]
    value_rows = projected[:, HEADS + 1]
    scores = jnp.einsum("qhc,kc->hqk", queries, key_rows, preferred_element_type=F32) * score_scale
    causal = lax.broadcasted_iota(jnp.int32, (seq_len, seq_len), 0) >= lax.broadcasted_iota(
        jnp.int32, (seq_len, seq_len), 1
    )
    scores = jnp.where(causal[None], scores, MASKED)
    row_max = jnp.max(scores, axis=2, keepdims=True)
    raised = jnp.exp(scores - row_max)
    attention = raised / jnp.sum(raised, axis=2, keepdims=True)
    attention_b = attention.astype(BF16)
    context = jnp.einsum(
        "hqk,kc->qhc", attention_b, value_rows, preferred_element_type=F32
    ).astype(BF16)
    context_flat = context.reshape(seq_len, HEADS * head_dim)
    context_both = jnp.concatenate([context_flat, swap(context_flat, "c")], axis=0)
    attn_out = jnp.einsum("thc,hdc->td", context, out_blocks, preferred_element_type=F32)
    residual = (tokens.astype(F32) + attn_out).astype(BF16)
    normed_two, inverse_two = layer_norm(residual)
    main, extra = between_experts(contract(slots, normed_two.astype(BF16), 1, 0).astype(BF16))
    one, two = spread(main, extra)

    def near(first, second):
        return [first[0][s] for s in range(4)] + [second[0][0], second[1][0]]

    def far(first, second):
        return (
            [first[1][s] for s in range(4)]
            + [second[0][s] for s in (1, 2, 3)]
            + [second[1][s] for s in (1, 2, 3)]
        )

    near_rows = experts(near(one, two), near(cot_one, cot_two), inner, outer, 240)
    far_rows = experts(far(one, two), far(cot_one, cot_two), inner, outer, 400)
    back_one = (dict(enumerate(near_rows[:4])), dict(enumerate(far_rows[:4])))
    back_two = (
        {0: near_rows[4], 1: far_rows[4], 2: far_rows[5], 3: far_rows[6]},
        {0: near_rows[5], 1: far_rows[7], 2: far_rows[8], 3: far_rows[9]},
    )
    sum_one, sum_two = collect(back_one, back_two)
    back_main, back_extra = between_experts(jnp.concatenate([sum_one, sum_two], axis=0))
    cut = EXPERTS * MAIN
    back_rows = contract(slots[:cut], back_main, 0, 0) + contract(slots[cut:], back_extra, 0, 0)
    moe_grad = gate_score * back_rows
    grad_hidden = cotangent.astype(F32) + norm_back(normed_two, inverse_two, moe_grad)
    grad_hidden_b = grad_hidden.astype(BF16)
    hidden_both = jnp.concatenate([grad_hidden_b, swap(grad_hidden_b, "c")], axis=0)
    grad_context = jnp.einsum(
        "td,hdc->thc", grad_hidden_b, out_blocks, preferred_element_type=F32
    )
    grad_context_b = grad_context.astype(BF16)
    grad_attention = jnp.einsum(
        "qhc,kc->hqk", grad_context_b, value_rows, preferred_element_type=F32
    )
    grad_value = jnp.einsum("hqk,qhc->kc", attention_b, grad_context_b, preferred_element_type=F32)
    grad_scores = (
        attention
        * (grad_attention - jnp.sum(grad_attention * attention, axis=2, keepdims=True))
        * score_scale
    )
    grad_scores_b = grad_scores.astype(BF16)
    grad_query = jnp.einsum("hqk,kc->qhc", grad_scores_b, key_rows, preferred_element_type=F32)
    grad_key = jnp.einsum("hqk,qhc->kc", grad_scores_b, queries, preferred_element_type=F32)
    grad_qkv = jnp.concatenate([grad_query, grad_key[:, None], grad_value[:, None]], axis=1).astype(BF16)
    grads_flat = grad_qkv.reshape(seq_len, (HEADS + 2) * head_dim)
    grads_both = jnp.concatenate([grads_flat, swap(grads_flat, "c")], axis=0)
    core = lax.axis_index("c").astype(jnp.int32).reshape(1)
    terms = param_terms(
        core, normed_both, hidden_both, grads_both, context_both, (seq_len * devices) ** (-0.5), head_dim
    )
    attn_grad = jnp.sum(exchange(terms, CHIPS).astype(F32), axis=0)
    grad_normed = jnp.einsum("tjc,jdc->td", grad_qkv, project, preferred_element_type=F32)
    grad_tokens = (grad_hidden + norm_back(normed_one, inverse_one, grad_normed)).astype(BF16)
    return (grad_tokens, attn_grad)


def solution(mesh):
    fine = Mesh(mesh.devices.reshape(SIZES), AXES)
    rows = P(AXES, None)
    in_specs = (
        rows,
        P(DP, None),
        rows,
        rows,
        P(EX, None, None, DP),
        P(EX, DP, None),
        rows,
    )
    return jax.shard_map(
        per_device, mesh=fine, in_specs=in_specs, out_specs=(rows, rows), check_vma=False
    )
```

time: 587 us -> 479 us (0.82); the launches traced: 586 us -> 469 us
  blocking collectives: 105 us -> 0 us
  starting transfers between devices: 13.3 us -> 112 us
  matrix products: 93.1 us -> 17.2 us
  waiting for transfers between devices: 308 us -> 240 us
  Pallas kernels: 0 us -> 60.4 us
  local copies, waits for them, and re-layouts: 31 us -> 14.3 us
  between operations: 14 us -> 1.91 us
    all_gather x2 -> x0, waiting for transfers between devices: 130 us -> none  [the longest x1 91.8 us: per_device(): all_normed = lax.all_gather(normed_rows, DP, axis=0, tiled=True)]
    reduce_scatter x1 -> x0, waiting for transfers between devices: 109 us -> none  [per_device(): summed = lax.psum_scatter(partial_rows, DP, scatter_dimension=0, tiled=True)]
    all_to_all x3 -> x0, blocking collectives: 105 us -> none  [the longest x2 55.8 us: to_experts(): lax.all_to_all(buffer.reshape(EXPERTS, CAP, features), EX, split_axis=0,...]
    ppermute x0 -> x27, waiting for transfers between devices: none -> 93.5 us  [along_z(): return lax.ppermute(values, 'z', [(i, (i + shift) % 4) for i in range(4)])]
    dot_general x7 -> x4, matrix products: 76.2 us -> 2.95 us  [contract(): lax.dot_general(first_op, second_op, (((first_dim,), (second_dim,)), ((),...]
    pallas_call x0 -> x3, Pallas kernels: none -> 60.4 us  [the longest x2 55.6 us: experts(): pl.pallas_call(lambda *refs: expert_kernel(count, rows, tall, *refs), out...]
    ppermute x0 -> x27, starting transfers between devices: none -> 51.4 us  [along_z(): return lax.ppermute(values, 'z', [(i, (i + shift) % 4) for i in range(4)])]
    ppermute x2 -> x20, waiting for transfers between devices: 9.15 us -> 59.8 us  [swap(): return lax.ppermute(values, axis, [(0, 1), (1, 0)])]
  transfers between devices with their start and end apart: 8 -> 52, of which waited for: 8 -> 24; matrix products, arithmetic and copies ran while one was open for 5% -> 9% of each run, Pallas kernels for 0% -> 5%
where the time goes in v2:
time: 479 us; the launch traced here: 469 us
  waiting for transfers between devices  240 us (50%)
  starting transfers between devices  112 us (23%)
  Pallas kernels  60.4 us (13%)
  other arithmetic  22.9 us (5%)
  matrix products  17.2 us (4%)
  local copies, waits for them, and re-layouts  14.3 us (3%)
    ppermute x27, waiting for transfers between devices, along_z(): return lax.ppermute(values, 'z', [(i, (i + shift) % 4) for i in range(4)])  93.5 us
    all_to_all x5, waiting for transfers between devices, exchange(): return lax.all_to_all(blocks, axes, split_axis=0, concat_axis=0, tiled=True)  86.9 us
    ppermute x20, waiting for transfers between devices, swap(): return lax.ppermute(values, axis, [(0, 1), (1, 0)])  59.8 us
    pallas_call x2, Pallas kernels, experts(): pl.pallas_call(lambda *refs: expert_kernel(count, rows, tall, *refs), out...  55.6 us
    ppermute x27, starting transfers between devices, along_z(): return lax.ppermute(values, 'z', [(i, (i + shift) % 4) for i in range(4)])  51.4 us
    all_to_all x5, starting transfers between devices, exchange(): return lax.all_to_all(blocks, axes, split_axis=0, concat_axis=0, tiled=True)  31.2 us
    ppermute x20, starting transfers between devices, swap(): return lax.ppermute(values, axis, [(0, 1), (1, 0)])  29.7 us
  transfers between devices with their start and end apart: 52, of which 24 were waited for; matrix products, arithmetic and copies ran while one was open for 9% of the time, Pallas kernels for 5%

profile of v2, /device:TPU:0, one launch (start us, length us, event | category | flops | bytes accessed | tf_op | source)
XLA Modules:
  0.0 469.3 jit_solution(4819362413524305023)
XLA Ops:
  3.4 8.2 %all-to-all-start = ((bf16[8,1152,128]{2,1,0:T(8,128)(2,1)}), bf16[8,1152,128]{2,1,0:T(8,128)(2,1)S(1)}, u32[]{:S(2)}, u32[]{:S(2)}) async-start(bf16[8,1152,128]{2,1,0:T(8,128)(2,1)} %broadcast_in_dim.14), calls=%async_computation | async-start | bytes 4718592 | tf_op jit(solution)/shard_map/all_to_all | solution.py:57
  13.2 29.7 %all-to-all-done = bf16[8,1152,128]{2,1,0:T(8,128)(2,1)S(1)} async-done(((bf16[8,1152,128]{2,1,0:T(8,128)(2,1)}), bf16[8,1152,128]{2,1,0:T(8,128)(2,1)S(1)}, u32[]{:S(2)}, u32[]{:S(2)}) %all-to-all-start) | async-done | bytes 2359328 | tf_op jit(solution)/shard_map/all_to_all | solution.py:57
  47.3 4.7 all-to-all-start.2
  53.8 14.0 %all-to-all-done.2 = bf16[16,8,3840]{2,1,0:T(8,128)(2,1)} async-done(((bf16[16,8,3840]{2,1,0:T(8,128)(2,1)}), bf16[16,8,3840]{2,1,0:T(8,128)(2,1)}, u32[]{:S(2)}, u32[]{:S(2)}) %all-to-all-start.2) | async-done | bytes 983072 | tf_op jit(solution)/shard_map/all_to_all | solution.py:57
  85.3 3.6 all-to-all-start.1
  99.0 6.9 %collective-permute-done.5.refs_7_ = bf16[80,3072]{1,0:T(8,128)(2,1)} collective-permute-done((bf16[80,3072]{1,0:T(8,128)(2,1)}, bf16[80,3072]{1,0:T(8,128)(2,1)}, u32[]{:S(2)}, u32[]{:S(2)}) %collective-permute-start.5) | collective-permute-done | bytes 491552 | tf_op jit(solution)/shard_map/ppermute | solution.py:53
  107.0 7.3 %collective-permute-done.8.refs_11_ = bf16[80,3072]{1,0:T(8,128)(2,1)} collective-permute-done((bf16[80,3072]{1,0:T(8,128)(2,1)}, bf16[80,3072]{1,0:T(8,128)(2,1)}, u32[]{:S(2)}, u32[]{:S(2)}) %collective-permute-start.8) | collective-permute-done | bytes 491552 | tf_op jit(solution)/shard_map/ppermute | solution.py:49
  116.7 8.1 %collective-permute-done.19.refs_10_ = bf16[80,3072]{1,0:T(8,128)(2,1)S(1)} collective-permute-done((bf16[80,3072]{1,0:T(8,128)(2,1)}, bf16[80,3072]{1,0:T(8,128)(2,1)S(1)}, u32[]{:S(2)}, u32[]{:S(2)}) %collective-permute-start.19) | collective-permute-done | bytes 491552 | tf_op jit(solution)/shard_map/ppermute | solution.py:49
  124.9 10.5 %collective-permute-done.22.refs_13_ = bf16[80,3072]{1,0:T(8,128)(2,1)} collective-permute-done((bf16[80,3072]{1,0:T(8,128)(2,1)}, bf16[80,3072]{1,0:T(8,128)(2,1)}, u32[]{:S(2)}, u32[]{:S(2)}) %collective-permute-start.22) | collective-permute-done | bytes 491552 | tf_op jit(solution)/shard_map/ppermute | solution.py:49
  137.6 8.2 %collective-permute-done.21.refs_12_ = bf16[80,3072]{1,0:T(8,128)(2,1)} collective-permute-done((bf16[80,3072]{1,0:T(8,128)(2,1)}, bf16[80,3072]{1,0:T(8,128)(2,1)}, u32[]{:S(2)}, u32[]{:S(2)}) %collective-permute-start.21) | collective-permute-done | bytes 491552 | tf_op jit(solution)/shard_map/ppermute | solution.py:49
  157.0 17.8 %collective-permute-done.3.refs_3_ = bf16[80,3072]{1,0:T(8,128)(2,1)S(1)} collective-permute-done((bf16[80,3072]{1,0:T(8,128)(2,1)S(1)}, bf16[80,3072]{1,0:T(8,128)(2,1)S(1)}, u32[]{:S(2)}, u32[]{:S(2)}) %collective-permute-start.3) | collective-permute-done | bytes 491552 | tf_op jit(solution)/shard_map/ppermute | solution.py:53
  179.5 14.2 %collective-permute-done.26.refs_17_ = bf16[80,3072]{1,0:T(8,128)(2,1)S(1)} collective-permute-done((bf16[80,3072]{1,0:T(8,128)(2,1)}, bf16[80,3072]{1,0:T(8,128)(2,1)S(1)}, u32[]{:S(2)}, u32[]{:S(2)}) %collective-permute-start.26) | collective-permute-done | bytes 491552 | tf_op jit(solution)/shard_map/ppermute | solution.py:53
  197.4 9.3 %collective-permute-start.13 = (bf16[80,3072]{1,0:T(8,128)(2,1)S(1)}, bf16[80,3072]{1,0:T(8,128)(2,1)S(1)}, u32[]{:S(2)}, u32[]{:S(2)}) collective-permute-start(bf16[80,3072]{1,0:T(8,128)(2,1)S(1)} %pad_maximum_fusion.7.refs_4_), channel_id=1, source_target_pairs={{0,32},{32,64},{64,96},{96,0},{1,33},{33,65},{65,97},{97,1},{2,34}... | collective-permute-start | bytes 1474568 | tf_op jit(solution)/shard_map/ppermute | solution.py:53
  207.4 6.0 %collective-permute-start.18 = (bf16[80,3072]{1,0:T(8,128)(2,1)S(1)}, bf16[80,3072]{1,0:T(8,128)(2,1)S(1)}, u32[]{:S(2)}, u32[]{:S(2)}) collective-permute-start(bf16[80,3072]{1,0:T(8,128)(2,1)S(1)} %collective-permute-done.4.refs_5_), channel_id=1, source_target_pairs={{0,96},{32,0},{64,32},{96,64},{1,97},{33,1},{65,33},{97,65},{2,98}... | collective-permute-start | bytes 1474568 | tf_op jit(solution)/shard_map/ppermute | solution.py:53
  219.5 3.6 collective-permute-start.10
  223.2 5.4 %collective-permute-done.13.refs_4_ = bf16[80,3072]{1,0:T(8,128)(2,1)S(1)} collective-permute-done((bf16[80,3072]{1,0:T(8,128)(2,1)S(1)}, bf16[80,3072]{1,0:T(8,128)(2,1)S(1)}, u32[]{:S(2)}, u32[]{:S(2)}) %collective-permute-start.13) | collective-permute-done | bytes 491552 | tf_op jit(solution)/shard_map/ppermute | solution.py:53
  228.6 3.9 collective-permute-done.18.refs_9_
  234.1 5.6 %collective-permute-done.16.refs_7_ = bf16[80,3072]{1,0:T(8,128)(2,1)S(1)} collective-permute-done((bf16[80,3072]{1,0:T(8,128)(2,1)S(1)}, bf16[80,3072]{1,0:T(8,128)(2,1)S(1)}, u32[]{:S(2)}, u32[]{:S(2)}) %collective-permute-start.16) | collective-permute-done | bytes 491552 | tf_op jit(solution)/shard_map/ppermute | solution.py:53
  240.5 31.8 %shard_map.87 = (bf16[80,3072]{1,0:T(8,128)(2,1)S(1)}, bf16[80,3072]{1,0:T(8,128)(2,1)S(1)}, bf16[80,3072]{1,0:T(8,128)(2,1)S(1)}, bf16[80,3072]{1,0:T(8,128)(2,...) custom-call(bf16[80,3072]{1,0:T(8,128)(2,1)S(1)} %collective-permute, ...), custom_call_target="tpu_custom_call" | custom-call | flops 16515072000 | bytes 27131904 | tf_op jit(solution)/shard_map/pallas_call | solution.py:218
  274.0 23.8 %shard_map.86 = (bf16[80,3072]{1,0:T(8,128)(2,1)S(1)}, bf16[80,3072]{1,0:T(8,128)(2,1)S(1)}, bf16[80,3072]{1,0:T(8,128)(2,1)S(1)}, bf16[80,3072]{1,0:T(8,128)(2,...) custom-call(bf16[80,3072]{1,0:T(8,128)(2,1)S(1)} %slice.98.refs_0_, ...), custom_call_target="tpu_custom_call" | custom-call | flops 9909043200 | bytes 21233664 | tf_op jit(solution)/shard_map/pallas_call | solution.py:218
  304.9 16.4 %collective-permute-done.39 = bf16[80,3072]{1,0:T(8,128)(2,1)S(1)} collective-permute-done((bf16[80,3072]{1,0:T(8,128)(2,1)S(1)}, bf16[80,3072]{1,0:T(8,128)(2,1)S(1)}, u32[]{:S(2)}, u32[]{:S(2)}) %collective-permute-start.39) | collective-permute-done | bytes 491552 | tf_op jit(solution)/shard_map/ppermute | solution.py:49
  323.4 8.5 %collective-permute-done.41 = bf16[80,3072]{1,0:T(8,128)(2,1)S(1)} collective-permute-done((bf16[80,3072]{1,0:T(8,128)(2,1)S(1)}, bf16[80,3072]{1,0:T(8,128)(2,1)S(1)}, u32[]{:S(2)}, u32[]{:S(2)}) %collective-permute-start.41) | collective-permute-done | bytes 491552 | tf_op jit(solution)/shard_map/ppermute | solution.py:49
  337.3 10.4 %collective-permute-done.31 = bf16[80,3072]{1,0:T(8,128)(2,1)S(1)} collective-permute-done((bf16[80,3072]{1,0:T(8,128)(2,1)S(1)}, bf16[80,3072]{1,0:T(8,128)(2,1)S(1)}, u32[]{:S(2)}, u32[]{:S(2)}) %collective-permute-start.31) | collective-permute-done | bytes 491552 | tf_op jit(solution)/shard_map/ppermute | solution.py:53
  352.2 6.7 %collective-permute-done.38 = bf16[80,3072]{1,0:T(8,128)(2,1)S(1)} collective-permute-done((bf16[80,3072]{1,0:T(8,128)(2,1)S(1)}, bf16[80,3072]{1,0:T(8,128)(2,1)S(1)}, u32[]{:S(2)}, u32[]{:S(2)}) %collective-permute-start.38) | collective-permute-done | bytes 491552 | tf_op jit(solution)/shard_map/ppermute | solution.py:53
  364.6 4.2 collective-permute-done.42
  369.2 9.4 %collective-permute-done.34 = bf16[80,3072]{1,0:T(8,128)(2,1)S(1)} collective-permute-done((bf16[80,3072]{1,0:T(8,128)(2,1)S(1)}, bf16[80,3072]{1,0:T(8,128)(2,1)S(1)}, u32[]{:S(2)}, u32[]{:S(2)}) %collective-permute-start.34) | collective-permute-done | bytes 491552 | tf_op jit(solution)/shard_map/ppermute | solution.py:53
  378.6 5.3 %collective-permute-done.35 = bf16[80,3072]{1,0:T(8,128)(2,1)S(1)} collective-permute-done((bf16[80,3072]{1,0:T(8,128)(2,1)S(1)}, bf16[80,3072]{1,0:T(8,128)(2,1)S(1)}, u32[]{:S(2)}, u32[]{:S(2)}) %collective-permute-start.35) | collective-permute-done | bytes 491552 | tf_op jit(solution)/shard_map/ppermute | solution.py:53
  385.5 4.8 %all-to-all-start.3 = ((bf16[16,8,3840]{2,1,0:T(8,128)(2,1)}), bf16[16,8,3840]{2,1,0:T(8,128)(2,1)S(1)}, u32[]{:S(2)}, u32[]{:S(2)}) async-start(bf16[16,8,3840]{2,1,0:T(8,128)(2,1)} %pad_maximum_fusion.5), calls=%async_computation.3 | async-start | bytes 1966080 | tf_op jit(solution)/shard_map/all_to_all | solution.py:57
  391.2 15.0 %all-to-all-done.3 = bf16[16,8,3840]{2,1,0:T(8,128)(2,1)S(1)} async-done(((bf16[16,8,3840]{2,1,0:T(8,128)(2,1)}), bf16[16,8,3840]{2,1,0:T(8,128)(2,1)S(1)}, u32[]{:S(2)}, u32[]{:S(2)}) %all-to-all-start.3) | async-done | bytes 983072 | tf_op jit(solution)/shard_map/all_to_all | solution.py:57
  418.4 4.8 %shard_map.88 = bf16[64,144,128]{2,1,0:T(8,128)(2,1)} custom-call(s32[1]{0:T(128)} %bitcast.34.refs_0_, bf16[256,3072]{1,0:T(8,128)(2,1)S(1)} %pad_maximum_fusion.1.refs_1_, bf16[256,3072]{1,0:T(8,128)(2,1)S(1)} %pad_maximum_fusion.2.refs_2_, bf16[256,512]{1,0:T(8,128)(2,1)S(1)} %pad_maximum_fusion.9.refs_3_, bf16[256,256]{1,0:T(8,128)(2,1)S(1)} %pad_maximum_fusion.10.refs_4_), custom_call_target="tpu_custom_call" | custom-call | flops 1207959552 | bytes 8388608 | tf_op jit(solution)/shard_map/pallas_call | solution.py:267
  423.2 9.9 %all-to-all-start.4 = ((bf16[64,144,128]{2,1,0:T(8,128)(2,1)}), bf16[64,144,128]{2,1,0:T(8,128)(2,1)}, u32[]{:S(2)}, u32[]{:S(2)}) async-start(bf16[64,144,128]{2,1,0:T(8,128)(2,1)} %shard_map.88), calls=%async_computation.4 | async-start | bytes 4718592 | tf_op jit(solution)/shard_map/all_to_all | solution.py:57
  438.0 28.2 %all-to-all-done.4 = bf16[64,144,128]{2,1,0:T(8,128)(2,1)} async-done(((bf16[64,144,128]{2,1,0:T(8,128)(2,1)}), bf16[64,144,128]{2,1,0:T(8,128)(2,1)}, u32[]{:S(2)}, u32[]{:S(2)}) %all-to-all-start.4) | async-done | bytes 2359328 | tf_op jit(solution)/shard_map/all_to_all | solution.py:57
  (229 shorter events, 121.0 us)
Async XLA Ops:
  3.4 39.4 %all-to-all-start = ((bf16[8,1152,128]{2,1,0:T(8,128)(2,1)}), bf16[8,1152,128]{2,1,0:T(8,128)(2,1)S(1)}, u32[]{:S(2)}, u32[]{:S(2)}) async-start(bf16[8,1152,128]{2,1,0:T(8,128)(2,1)} %broadcast_in_dim.14), calls=%async_computation | async-start | bytes 4718592 | tf_op jit(solution)/shard_map/all_to_all | solution.py:57
  42.9 29.1 %collective-permute-start = (bf16[8,1152,128]{2,1,0:T(8,128)(2,1)S(1)}, bf16[8,1152,128]{2,1,0:T(8,128)(2,1)}, u32[]{:S(2)}, u32[]{:S(2)}) collective-permute-start(bf16[8,1152,128]{2,1,0:T(8,128)(2,1)S(1)} %all-to-all-done), channel_id=1, source_target_pairs={{0,1},{1,0},{2,3},{3,2},{4,5},{5,4},{6,7},{7,6},{8,9},{9,8},{10,11... | collective-permute-start | bytes 7077896 | tf_op jit(solution)/shard_map/ppermute | solution.py:49
  69.7 25.7 %collective-permute-start.7 = (bf16[80,3072]{1,0:T(8,128)(2,1)}, bf16[80,3072]{1,0:T(8,128)(2,1)}, u32[]{:S(2)}, u32[]{:S(2)}) collective-permute-start(bf16[80,3072]{1,0:T(8,128)(2,1)} %slice.103.refs_6_), channel_id=1, source_target_pairs={{0,96},{32,0},{64,32},{96,64},{1,97},{33,1},{65,33},{97,65},{2,98}... | collective-permute-start | bytes 1474568 | tf_op jit(solution)/shard_map/ppermute | solution.py:53
  71.2 26.0 %collective-permute-start.6 = (bf16[80,3072]{1,0:T(8,128)(2,1)}, bf16[80,3072]{1,0:T(8,128)(2,1)}, u32[]{:S(2)}, u32[]{:S(2)}) collective-permute-start(bf16[80,3072]{1,0:T(8,128)(2,1)} %slice.103.refs_6_), channel_id=1, source_target_pairs={{0,64},{32,96},{64,0},{96,32},{1,65},{33,97},{65,1},{97,33},{2,66}... | collective-permute-start | bytes 1474568 | tf_op jit(solution)/shard_map/ppermute | solution.py:53
  85.3 31.4 %all-to-all-start.1 = ((bf16[16,8,3840]{2,1,0:T(8,128)(2,1)}), bf16[16,8,3840]{2,1,0:T(8,128)(2,1)S(1)}, u32[]{:S(2)}, u32[]{:S(2)}) async-start(bf16[16,8,3840]{2,1,0:T(8,128)(2,1)} %pad_maximum_fusion.3), calls=%async_computation.1 | async-start | bytes 1966080 | tf_op jit(solution)/shard_map/all_to_all | solution.py:57
  91.9 22.5 %collective-permute-start.8 = (bf16[80,3072]{1,0:T(8,128)(2,1)}, bf16[80,3072]{1,0:T(8,128)(2,1)}, u32[]{:S(2)}, u32[]{:S(2)}) collective-permute-start(bf16[80,3072]{1,0:T(8,128)(2,1)} %pad_maximum_fusion.8.refs_10_), channel_id=1, source_target_pairs={{0,16},{16,0},{1,17},{17,1},{2,18},{18,2},{3,19},{19,3},{4,20},{20... | collective-permute-start | bytes 1474568 | tf_op jit(solution)/shard_map/ppermute | solution.py:49
  93.6 31.2 %collective-permute-start.19 = (bf16[80,3072]{1,0:T(8,128)(2,1)}, bf16[80,3072]{1,0:T(8,128)(2,1)S(1)}, u32[]{:S(2)}, u32[]{:S(2)}) collective-permute-start(bf16[80,3072]{1,0:T(8,128)(2,1)} %slice.103.refs_6_), channel_id=1, source_target_pairs={{0,16},{16,0},{1,17},{17,1},{2,18},{18,2},{3,19},{19,3},{4,20},{20... | collective-permute-start | bytes 1474568 | tf_op jit(solution)/shard_map/ppermute | solution.py:49
  95.4 40.0 %collective-permute-start.22 = (bf16[80,3072]{1,0:T(8,128)(2,1)}, bf16[80,3072]{1,0:T(8,128)(2,1)}, u32[]{:S(2)}, u32[]{:S(2)}) collective-permute-start(bf16[80,3072]{1,0:T(8,128)(2,1)} %collective-permute-done.7.refs_9_), channel_id=1, source_target_pairs={{0,16},{16,0},{1,17},{17,1},{2,18},{18,2},{3,19},{19,3},{4,20},{20... | collective-permute-start | bytes 1474568 | tf_op jit(solution)/shard_map/ppermute | solution.py:49
  97.2 48.7 %collective-permute-start.21 = (bf16[80,3072]{1,0:T(8,128)(2,1)}, bf16[80,3072]{1,0:T(8,128)(2,1)}, u32[]{:S(2)}, u32[]{:S(2)}) collective-permute-start(bf16[80,3072]{1,0:T(8,128)(2,1)} %collective-permute-done.6.refs_8_), channel_id=1, source_target_pairs={{0,16},{16,0},{1,17},{17,1},{2,18},{18,2},{3,19},{19,3},{4,20},{20... | collective-permute-start | bytes 1474568 | tf_op jit(solution)/shard_map/ppermute | solution.py:49
  105.8 42.2 %collective-permute-start.25 = (bf16[80,3072]{1,0:T(8,128)(2,1)}, bf16[80,3072]{1,0:T(8,128)(2,1)}, u32[]{:S(2)}, u32[]{:S(2)}) collective-permute-start(bf16[80,3072]{1,0:T(8,128)(2,1)} %pad_maximum_fusion.8.refs_10_), channel_id=1, source_target_pairs={{0,96},{32,0},{64,32},{96,64},{1,97},{33,1},{65,33},{97,65},{2,98}... | collective-permute-start | bytes 1474568 | tf_op jit(solution)/shard_map/ppermute | solution.py:53
  114.4 36.5 %collective-permute-start.24 = (bf16[80,3072]{1,0:T(8,128)(2,1)}, bf16[80,3072]{1,0:T(8,128)(2,1)}, u32[]{:S(2)}, u32[]{:S(2)}) collective-permute-start(bf16[80,3072]{1,0:T(8,128)(2,1)} %pad_maximum_fusion.8.refs_10_), channel_id=1, source_target_pairs={{0,64},{32,96},{64,0},{96,32},{1,65},{33,97},{65,1},{97,33},{2,66}... | collective-permute-start | bytes 1474568 | tf_op jit(solution)/shard_map/ppermute | solution.py:53
  124.8 28.1 %collective-permute-start.23 = (bf16[80,3072]{1,0:T(8,128)(2,1)}, bf16[80,3072]{1,0:T(8,128)(2,1)}, u32[]{:S(2)}, u32[]{:S(2)}) collective-permute-start(bf16[80,3072]{1,0:T(8,128)(2,1)} %pad_maximum_fusion.8.refs_10_), channel_id=1, source_target_pairs={{0,32},{32,64},{64,96},{96,0},{1,33},{33,65},{65,97},{97,1},{2,34}... | collective-permute-start | bytes 1474568 | tf_op jit(solution)/shard_map/ppermute | solution.py:53
  145.8 29.0 %collective-permute-start.3 = (bf16[80,3072]{1,0:T(8,128)(2,1)S(1)}, bf16[80,3072]{1,0:T(8,128)(2,1)S(1)}, u32[]{:S(2)}, u32[]{:S(2)}) collective-permute-start(bf16[80,3072]{1,0:T(8,128)(2,1)S(1)} %slice.98.refs_0_), channel_id=1, source_target_pairs={{0,96},{32,0},{64,32},{96,64},{1,97},{33,1},{65,33},{97,65},{2,98}... | collective-permute-start | bytes 1474568 | tf_op jit(solution)/shard_map/ppermute | solution.py:53
  148.1 27.8 %collective-permute-start.1 = (bf16[80,3072]{1,0:T(8,128)(2,1)S(1)}, bf16[80,3072]{1,0:T(8,128)(2,1)S(1)}, u32[]{:S(2)}, u32[]{:S(2)}) collective-permute-start(bf16[80,3072]{1,0:T(8,128)(2,1)S(1)} %slice.98.refs_0_), channel_id=1, source_target_pairs={{0,32},{32,64},{64,96},{96,0},{1,33},{33,65},{65,97},{97,1},{2,34}... | collective-permute-start | bytes 1474568 | tf_op jit(solution)/shard_map/ppermute | solution.py:53
  150.8 25.2 %collective-permute-start.27 = (bf16[80,3072]{1,0:T(8,128)(2,1)}, bf16[80,3072]{1,0:T(8,128)(2,1)S(1)}, u32[]{:S(2)}, u32[]{:S(2)}) collective-permute-start(bf16[80,3072]{1,0:T(8,128)(2,1)} %collective-permute-done.8.refs_11_), channel_id=1, source_target_pairs={{0,64},{32,96},{64,0},{96,32},{1,65},{33,97},{65,1},{97,33},{2,66}... | collective-permute-start | bytes 1474568 | tf_op jit(solution)/shard_map/ppermute | solution.py:53
  152.9 40.8 %collective-permute-start.26 = (bf16[80,3072]{1,0:T(8,128)(2,1)}, bf16[80,3072]{1,0:T(8,128)(2,1)S(1)}, u32[]{:S(2)}, u32[]{:S(2)}) collective-permute-start(bf16[80,3072]{1,0:T(8,128)(2,1)} %collective-permute-done.8.refs_11_), channel_id=1, source_target_pairs={{0,32},{32,64},{64,96},{96,0},{1,33},{33,65},{65,97},{97,1},{2,34}... | collective-permute-start | bytes 1474568 | tf_op jit(solution)/shard_map/ppermute | solution.py:53
  154.9 42.4 %collective-permute-start.20 = (bf16[80,3072]{1,0:T(8,128)(2,1)}, bf16[80,3072]{1,0:T(8,128)(2,1)S(1)}, u32[]{:S(2)}, u32[]{:S(2)}) collective-permute-start(bf16[80,3072]{1,0:T(8,128)(2,1)} %collective-permute-done.5.refs_7_), channel_id=1, source_target_pairs={{0,16},{16,0},{1,17},{17,1},{2,18},{18,2},{3,19},{19,3},{4,20},{20... | collective-permute-start | bytes 1474568 | tf_op jit(solution)/shard_map/ppermute | solution.py:49
  197.4 31.2 %collective-permute-start.13 = (bf16[80,3072]{1,0:T(8,128)(2,1)S(1)}, bf16[80,3072]{1,0:T(8,128)(2,1)S(1)}, u32[]{:S(2)}, u32[]{:S(2)}) collective-permute-start(bf16[80,3072]{1,0:T(8,128)(2,1)S(1)} %pad_maximum_fusion.7.refs_4_), channel_id=1, source_target_pairs={{0,32},{32,64},{64,96},{96,0},{1,33},{33,65},{65,97},{97,1},{2,34}... | collective-permute-start | bytes 1474568 | tf_op jit(solution)/shard_map/ppermute | solution.py:53
  207.4 25.1 %collective-permute-start.18 = (bf16[80,3072]{1,0:T(8,128)(2,1)S(1)}, bf16[80,3072]{1,0:T(8,128)(2,1)S(1)}, u32[]{:S(2)}, u32[]{:S(2)}) collective-permute-start(bf16[80,3072]{1,0:T(8,128)(2,1)S(1)} %collective-permute-done.4.refs_5_), channel_id=1, source_target_pairs={{0,96},{32,0},{64,32},{96,64},{1,97},{33,1},{65,33},{97,65},{2,98}... | collective-permute-start | bytes 1474568 | tf_op jit(solution)/shard_map/ppermute | solution.py:53
  216.2 23.5 %collective-permute-start.16 = (bf16[80,3072]{1,0:T(8,128)(2,1)S(1)}, bf16[80,3072]{1,0:T(8,128)(2,1)S(1)}, u32[]{:S(2)}, u32[]{:S(2)}) collective-permute-start(bf16[80,3072]{1,0:T(8,128)(2,1)S(1)} %collective-permute-done.4.refs_5_), channel_id=1, source_target_pairs={{0,32},{32,64},{64,96},{96,0},{1,33},{33,65},{65,97},{97,1},{2,34}... | collective-permute-start | bytes 1474568 | tf_op jit(solution)/shard_map/ppermute | solution.py:53
  272.4 31.0 %collective-permute-start.37 = (bf16[80,3072]{1,0:T(8,128)(2,1)S(1)}, bf16[80,3072]{1,0:T(8,128)(2,1)S(1)}, u32[]{:S(2)}, u32[]{:S(2)}) collective-permute-start(bf16[80,3072]{1,0:T(8,128)(2,1)S(1)} %get-tuple-element.37), channel_id=1, source_target_pairs={{0,16},{16,0},{1,17},{17,1},{2,18},{18,2},{3,19},{19,3},{4,20},{20... | collective-permute-start | bytes 1474568 | tf_op jit(solution)/shard_map/ppermute | solution.py:49
  297.9 71.3 %collective-permute-start.33 = (bf16[80,3072]{1,0:T(8,128)(2,1)S(1)}, bf16[80,3072]{1,0:T(8,128)(2,1)S(1)}, u32[]{:S(2)}, u32[]{:S(2)}) collective-permute-start(bf16[80,3072]{1,0:T(8,128)(2,1)S(1)} %get-tuple-element.31), channel_id=1, source_target_pairs={{0,96},{32,0},{64,32},{96,64},{1,97},{33,1},{65,33},{97,65},{2,98}... | collective-permute-start | bytes 1474568 | tf_op jit(solution)/shard_map/ppermute | solution.py:53
  299.2 51.3 %collective-permute-start.36 = (bf16[80,3072]{1,0:T(8,128)(2,1)S(1)}, bf16[80,3072]{1,0:T(8,128)(2,1)S(1)}, u32[]{:S(2)}, u32[]{:S(2)}) collective-permute-start(bf16[80,3072]{1,0:T(8,128)(2,1)S(1)} %get-tuple-element.35), channel_id=1, source_target_pairs={{0,16},{16,0},{1,17},{17,1},{2,18},{18,2},{3,19},{19,3},{4,20},{20... | collective-permute-start | bytes 1474568 | tf_op jit(solution)/shard_map/ppermute | solution.py:49
  301.3 33.4 %collective-permute-start.29 = (bf16[80,3072]{1,0:T(8,128)(2,1)S(1)}, bf16[80,3072]{1,0:T(8,128)(2,1)S(1)}, u32[]{:S(2)}, u32[]{:S(2)}) collective-permute-start(bf16[80,3072]{1,0:T(8,128)(2,1)S(1)} %get-tuple-element.28), channel_id=1, source_target_pairs={{0,96},{32,0},{64,32},{96,64},{1,97},{33,1},{65,33},{97,65},{2,98}... | collective-permute-start | bytes 1474568 | tf_op jit(solution)/shard_map/ppermute | solution.py:53
  302.4 34.9 %collective-permute-start.30 = (bf16[80,3072]{1,0:T(8,128)(2,1)S(1)}, bf16[80,3072]{1,0:T(8,128)(2,1)S(1)}, u32[]{:S(2)}, u32[]{:S(2)}) collective-permute-start(bf16[80,3072]{1,0:T(8,128)(2,1)S(1)} %get-tuple-element.29), channel_id=1, source_target_pairs={{0,32},{32,64},{64,96},{96,0},{1,33},{33,65},{65,97},{97,1},{2,34}... | collective-permute-start | bytes 1474568 | tf_op jit(solution)/shard_map/ppermute | solution.py:53
  334.7 24.1 %collective-permute-start.38 = (bf16[80,3072]{1,0:T(8,128)(2,1)S(1)}, bf16[80,3072]{1,0:T(8,128)(2,1)S(1)}, u32[]{:S(2)}, u32[]{:S(2)}) collective-permute-start(bf16[80,3072]{1,0:T(8,128)(2,1)S(1)} %add_convert_fusion.3), channel_id=1, source_target_pairs={{0,96},{32,0},{64,32},{96,64},{1,97},{33,1},{65,33},{97,65},{2,98}... | collective-permute-start | bytes 1474568 | tf_op jit(solution)/shard_map/ppermute | solution.py:53
  337.3 25.9 %collective-permute-start.40 = (bf16[80,3072]{1,0:T(8,128)(2,1)S(1)}, bf16[80,3072]{1,0:T(8,128)(2,1)S(1)}, u32[]{:S(2)}, u32[]{:S(2)}) collective-permute-start(bf16[80,3072]{1,0:T(8,128)(2,1)S(1)} %add_convert_fusion.2), channel_id=1, source_target_pairs={{0,32},{32,64},{64,96},{96,0},{1,33},{33,65},{65,97},{97,1},{2,34}... | collective-permute-start | bytes 1474568 | tf_op jit(solution)/shard_map/ppermute | solution.py:53
  350.5 28.1 %collective-permute-start.34 = (bf16[80,3072]{1,0:T(8,128)(2,1)S(1)}, bf16[80,3072]{1,0:T(8,128)(2,1)S(1)}, u32[]{:S(2)}, u32[]{:S(2)}) collective-permute-start(bf16[80,3072]{1,0:T(8,128)(2,1)S(1)} %get-tuple-element.32), channel_id=1, source_target_pairs={{0,32},{32,64},{64,96},{96,0},{1,33},{33,65},{65,97},{97,1},{2,34}... | collective-permute-start | bytes 1474568 | tf_op jit(solution)/shard_map/ppermute | solution.py:53
  358.8 25.1 %collective-permute-start.35 = (bf16[80,3072]{1,0:T(8,128)(2,1)S(1)}, bf16[80,3072]{1,0:T(8,128)(2,1)S(1)}, u32[]{:S(2)}, u32[]{:S(2)}) collective-permute-start(bf16[80,3072]{1,0:T(8,128)(2,1)S(1)} %get-tuple-element.33), channel_id=1, source_target_pairs={{0,64},{32,96},{64,0},{96,32},{1,65},{33,97},{65,1},{97,33},{2,66}... | collective-permute-start | bytes 1474568 | tf_op jit(solution)/shard_map/ppermute | solution.py:53
  390.4 25.5 %collective-permute-start.43 = (bf16[128,3072]{1,0:T(8,128)(2,1)}, bf16[128,3072]{1,0:T(8,128)(2,1)}, u32[]{:S(2)}, u32[]{:S(2)}) collective-permute-start(bf16[128,3072]{1,0:T(8,128)(2,1)} %fusion.13), channel_id=1, source_target_pairs={{0,1},{1,0},{2,3},{3,2},{4,5},{5,4},{6,7},{7,6},{8,9},{9,8},{10,11... | collective-permute-start | bytes 2359304 | tf_op jit(solution)/shard_map/ppermute | solution.py:49
  390.9 26.2 %collective-permute-start.46 = (bf16[128,256]{1,0:T(8,128)(2,1)S(1)}, bf16[128,256]{1,0:T(8,128)(2,1)S(1)}, u32[]{:S(2)}, u32[]{:S(2)}) collective-permute-start(bf16[128,256]{1,0:T(8,128)(2,1)S(1)} %copy.35), channel_id=1, source_target_pairs={{0,1},{1,0},{2,3},{3,2},{4,5},{5,4},{6,7},{7,6},{8,9},{9,8},{10,11... | collective-permute-start | bytes 196616 | tf_op jit(solution)/shard_map/ppermute | solution.py:49
  423.2 43.0 %all-to-all-start.4 = ((bf16[64,144,128]{2,1,0:T(8,128)(2,1)}), bf16[64,144,128]{2,1,0:T(8,128)(2,1)}, u32[]{:S(2)}, u32[]{:S(2)}) async-start(bf16[64,144,128]{2,1,0:T(8,128)(2,1)} %shard_map.88), calls=%async_computation.4 | async-start | bytes 4718592 | tf_op jit(solution)/shard_map/all_to_all | solution.py:57
  (61 other events, 937.2 us)

commit v3 on v2

--- a/solution.py
+++ b/solution.py
@@ -82,12 +82,52 @@
     return (jnp.arange(EXPERTS * CAP, dtype=jnp.int32)[:, None] == target[None, :]).astype(BF16)
 
 
-def gather_params(attn_param):
+def place_kernel(places, piece, at_ref, *refs):
+    block_refs, out_ref, sems = refs[: len(places)], refs[-2], refs[-1]
+    copies = []
+    number = 0
+    for ref, parts in zip(block_refs, places):
+        for i, (s, r, half) in enumerate(parts):
+            z = lax.rem(at_ref[0] - s + 4, 4)
+            yh = lax.rem(at_ref[1] + r, 2)
+            copy = pltpu.make_async_copy(
+                ref.at[pl.ds(i * piece, piece)], out_ref.at[z * 2 + yh, pl.ds(half * piece, piece)], sems.at[number]
+            )
+            copy.start()
+            copies.append(copy)
+            number += 1
+    for copy in copies:
+        copy.wait()
+
+
+def gather_params(attn_param, earlier):
     rows, head_dim = attn_param.shape
     half = rows // 2
+    piece = half // 2
     core = lax.axis_index("c")
     own = lax.dynamic_slice_in_dim(attn_param, core * half, half, 0)
-    own = exchange(jnp.broadcast_to(own[None], (N_DP, half, head_dim)), DP)
+    first, second = own[:piece], own[piece:]
+    around = [along_z(first, s) for s in (1, 3, 2)]
+    own_y = swap(own, "yh")
+    pair = after(jnp.concatenate([second, own_y[piece:]], axis=0), around[0], around[1])
+    around_y = [swap(block, "yh") for block in around]
+    pairs = [along_z(pair, s) for s in (1, 3, 2)]
+    blocks = [own, own_y] + around + around_y + pairs
+    places = (
+        [[(0, 0, 0), (0, 0, 1)], [(0, 1, 0), (0, 1, 1)]]
+        + [[(s, 0, 0)] for s in (1, 3, 2)]
+        + [[(s, 1, 0)] for s in (1, 3, 2)]
+        + [[(s, 0, 1), (s, 1, 1)] for s in (1, 3, 2)]
+    )
+    at = after(jnp.stack([lax.axis_index("z"), lax.axis_index("yh")]).astype(jnp.int32), earlier)
+    anywhere = pl.BlockSpec(memory_space=pl.ANY)
+    own = pl.pallas_call(
+        lambda *refs: place_kernel(places, piece, *refs),
+        out_shape=jax.ShapeDtypeStruct((N_DP, half, head_dim), BF16),
+        in_specs=[pl.BlockSpec(memory_space=pltpu.SMEM)] + [anywhere] * len(blocks),
+        out_specs=anywhere,
+        scratch_shapes=[pltpu.SemaphoreType.DMA((16,))],
+    )(at, *blocks)
     other = swap(own, "c")
     first = jnp.where(core == 0, own, other)
     second = jnp.where(core == 0, other, own)
@@ -105,52 +145,61 @@
     return packed[:, :features], extra
 
 
-def spread(main, extra):
-    one = main[:HALF]
-    two = jnp.concatenate([main[HALF:], extra], axis=0)
-    one_z = {0: one, 1: along_z(one, 1), 3: along_z(one, -1), 2: along_z(one, 2)}
-    two_y = swap(two, "yh")
-    one_y = {0: swap(one, "yh")}
-    for s in (1, 3, 2):
-        one_y[s] = swap(one_z[s], "yh")
-    late, late_y = after(two, one_z[1], one_z[3]), after(two_y, one_z[1], one_z[3])
-    two_z, two_yz = {0: two}, {0: two_y}
-    for s in (1, 3, 2):
-        two_z[s] = along_z(late, s)
-    for s in (1, 3, 2):
-        two_yz[s] = along_z(late_y, s)
-    return (one_z, one_y), (two_z, two_yz)
-
-
-def collect(first, second):
-    early = [along_z(first[0][s], -s) for s in (1, 3, 2)]
-    early_y = swap(second[1][0], "yh")
-    late = [along_z(first[1][s], -s) for s in (1, 3, 2)]
-    swapped = {s: swap(second[1][s], "yh") for s in (1, 3, 2)}
-    far = add_round(first[1][0], *late)
-    far = swap(far, "yh")
-    back = [along_z(add_round(second[0][s], swapped[s]), -s) for s in (1, 3, 2)]
-    one = add_round(first[0][0], far, *early)
-    two = add_round(second[0][0], early_y, *back)
-    return one, two
-
-
-def expert_kernel(count, rows, tall, *refs):
+def spread_near(own):
+    one = own[:HALF]
+    own_y = swap(own, "yh")
+    return [own, own_y] + [along_z(one, s) for s in (1, 3, 2)]
+
+
+def spread_far(near, between):
+    own, own_y, near_z, far_z, across = near
+    pair = after(jnp.concatenate([own[HALF:], own_y[HALF:]], axis=0), near_z, far_z)
+    first = [swap(near_z, "yh"), swap(far_z, "yh")]
+    second = [along_z(pair, 1), along_z(pair, 3)]
+    return first + [swap(after(across, *between), "yh")] + second + [along_z(pair, 2)]
+
+
+def collect(near, far):
+    kept, one_y, two_y, *one_z = near
+    early = [along_z(block, -s) for block, s in zip(one_z, (1, 3, 2))]
+    early_y = swap(two_y, "yh")
+    *one_yz, two_z, two_yz = far
+    (*one_yz, two_yz), early, early_y = lax.optimization_barrier(([*one_yz, two_yz], early, early_y))
+    late = [along_z(block, -s) for block, s in zip(one_yz, (1, 3, 2))]
+    swapped = swap(two_yz, "yh")
+    across = swap(add_round(one_y, *late), "yh")
+    pairs = add_round(two_z, swapped)
+    back = [along_z(pairs[i * HALF : (i + 1) * HALF], -s) for i, s in enumerate((1, 3, 2))]
+    one = add_round(kept[:HALF], across, *early)
+    two = add_round(kept[HALF:], early_y, *back)
+    return jnp.concatenate([one, two], axis=0)
+
+
+def expert_kernel(counts, pieces_out, tall, *refs):
+    count = len(counts)
+    outs = len(pieces_out)
     normed_refs, cot_refs = refs[:count], refs[count : 2 * count]
     inner_ref, outer_ref = refs[2 * count : 2 * count + 2]
-    out_refs = refs[2 * count + 2 : 3 * count + 2]
+    out_refs = refs[2 * count + 2 : 2 * count + 2 + outs]
     (normed, cot, gate_map, up_map, outer_map, grad_gate, grad_up, result, row_sem, map_sem, out_sem) = refs[
-        3 * count + 2 :
+        2 * count + 2 + outs :
     ]
     hidden, features = outer_ref.shape
+    starts = [sum(counts[:i]) for i in range(count)]
 
     def load(source, target, sem):
         copy = pltpu.make_async_copy(source, target, sem)
         copy.start()
         return copy
 
+    def load_rows(block_refs, target, side):
+        return [
+            load(ref, target.at[pl.ds(starts[i], counts[i])], row_sem.at[side, i])
+            for i, ref in enumerate(block_refs)
+        ]
+
     pieces = [(0, 256), (256, 256), (512, hidden - 512)]
-    rows_in = [load(ref, normed.at[pl.ds(i * rows, rows)], row_sem.at[0, i]) for i, ref in enumerate(normed_refs)]
+    rows_in = load_rows(normed_refs, normed, 0)
     maps_in = []
     for i, (start, size) in enumerate(pieces):
         at = pl.ds(start, size)
@@ -162,15 +211,13 @@
             ]
         )
         if i == 0:
-            rows_in += [
-                load(ref, cot.at[pl.ds(j * rows, rows)], row_sem.at[1, j]) for j, ref in enumerate(cot_refs)
-            ]
+            rows_in += load_rows(cot_refs, cot, 1)
     blank = jnp.zeros((PADDED - hidden, features), BF16)
     for ref in (gate_map, up_map, outer_map):
         ref[pl.ds(hidden, PADDED - hidden)] = blank
     for copy in rows_in:
         copy.wait()
-    steps = count * rows // tall
+    steps = sum(counts) // tall
 
     for i in range(len(pieces)):
         for copy in maps_in[i]:
@@ -201,25 +248,36 @@
                 + contract(grad_up[here], up_map[:, lanes], 1, 0)
             ).astype(BF16)
 
-        copies += [
-            load(result.at[pl.ds(i * rows, rows), lanes], ref.at[:, lanes], out_sem.at[n, i])
-            for i, ref in enumerate(out_refs)
-        ]
+        number = 0
+        for ref, parts in zip(out_refs, pieces_out):
+            at = 0
+            for start, size in parts:
+                copies.append(
+                    load(
+                        result.at[pl.ds(start, size), lanes],
+                        ref.at[pl.ds(at, size), lanes],
+                        out_sem.at[n, number],
+                    )
+                )
+                at += size
+                number += 1
     for copy in copies:
         copy.wait()
 
 
-def experts(normed_blocks, cot_blocks, inner, outer, tall):
-    count = len(normed_blocks)
-    rows, features = normed_blocks[0].shape
+def experts(normed_blocks, cot_blocks, inner, outer, pieces_out, tall):
+    counts = [block.shape[0] for block in normed_blocks]
+    features = normed_blocks[0].shape[1]
     hidden = outer.shape[0]
-    total = count * rows
+    total = sum(counts)
     anywhere = pl.BlockSpec(memory_space=pl.ANY)
     return pl.pallas_call(
-        lambda *refs: expert_kernel(count, rows, tall, *refs),
-        out_shape=[jax.ShapeDtypeStruct((rows, features), BF16)] * count,
-        in_specs=[anywhere] * (2 * count + 2),
-        out_specs=[anywhere] * count,
+        lambda *refs: expert_kernel(counts, pieces_out, tall, *refs),
+        out_shape=[
+            jax.ShapeDtypeStruct((sum(size for _, size in parts), features), BF16) for parts in pieces_out
+        ],
+        in_specs=[anywhere] * (2 * len(counts) + 2),
+        out_specs=[anywhere] * len(pieces_out),
         scratch_shapes=[
             pltpu.VMEM((total, features), BF16),
             pltpu.VMEM((total, features), BF16),
@@ -229,9 +287,9 @@
             pltpu.VMEM((total, PADDED), BF16),
             pltpu.VMEM((total, PADDED), BF16),
             pltpu.VMEM((total, features), BF16),
-            pltpu.SemaphoreType.DMA((2, count)),
+            pltpu.SemaphoreType.DMA((2, len(counts))),
             pltpu.SemaphoreType.DMA((3, 3)),
-            pltpu.SemaphoreType.DMA((features // 512, count)),
+            pltpu.SemaphoreType.DMA((features // 512, sum(len(parts) for parts in pieces_out))),
         ],
         compiler_params=pltpu.CompilerParams(vmem_limit_bytes=48 * 1024 * 1024),
         cost_estimate=pl.CostEstimate(
@@ -286,9 +344,10 @@
     inner = jnp.transpose(w_in[0], (1, 2, 0))
     outer = w_out[0]
 
-    packed = gather_params(attn_param)
     cot_main, cot_extra = between_experts(contract(slots, cotangent, 1, 0).astype(BF16))
-    cot_one, cot_two = spread(cot_main, cot_extra)
+    packed = gather_params(attn_param, cot_main)
+    cot_near = spread_near(jnp.concatenate([cot_main, cot_extra], axis=0))
+    cot_far = spread_far(cot_near, ())
 
     normed_one, inverse_one = layer_norm(tokens)
     normed_one_b = normed_one.astype(BF16)
@@ -320,27 +379,33 @@
     residual = (tokens.astype(F32) + attn_out).astype(BF16)
     normed_two, inverse_two = layer_norm(residual)
     main, extra = between_experts(contract(slots, normed_two.astype(BF16), 1, 0).astype(BF16))
-    one, two = spread(main, extra)
-
-    def near(first, second):
-        return [first[0][s] for s in range(4)] + [second[0][0], second[1][0]]
-
-    def far(first, second):
-        return (
-            [first[1][s] for s in range(4)]
-            + [second[0][s] for s in (1, 2, 3)]
-            + [second[1][s] for s in (1, 2, 3)]
-        )
-
-    near_rows = experts(near(one, two), near(cot_one, cot_two), inner, outer, 240)
-    far_rows = experts(far(one, two), far(cot_one, cot_two), inner, outer, 400)
-    back_one = (dict(enumerate(near_rows[:4])), dict(enumerate(far_rows[:4])))
-    back_two = (
-        {0: near_rows[4], 1: far_rows[4], 2: far_rows[5], 3: far_rows[6]},
-        {0: near_rows[5], 1: far_rows[7], 2: far_rows[8], 3: far_rows[9]},
-    )
-    sum_one, sum_two = collect(back_one, back_two)
-    back_main, back_extra = between_experts(jnp.concatenate([sum_one, sum_two], axis=0))
+    near = spread_near(after(jnp.concatenate([main, extra], axis=0), *cot_far))
+    near[4], normed_both, context_both = lax.optimization_barrier((near[4], normed_both, context_both))
+    h = HALF
+    near_rows = experts(
+        near,
+        cot_near,
+        inner,
+        outer,
+        [[(0, 2 * h)], [(2 * h, h)], [(3 * h, h)], [(4 * h, h)], [(5 * h, h)], [(6 * h, h)]],
+        7 * h,
+    )
+    far = spread_far(near, (near_rows[0],))
+    far_rows = experts(
+        far,
+        cot_far,
+        inner,
+        outer,
+        [
+            [(0, h)],
+            [(h, h)],
+            [(2 * h, h)],
+            [(3 * h, h), (5 * h, h), (7 * h, h)],
+            [(4 * h, h), (6 * h, h), (8 * h, h)],
+        ],
+        3 * h,
+    )
+    back_main, back_extra = between_experts(collect(near_rows, far_rows))
     cut = EXPERTS * MAIN
     back_rows = contract(slots[:cut], back_main, 0, 0) + contract(slots[cut:], back_extra, 0, 0)
     moe_grad = gate_score * back_rows

time: 479 us -> 491 us (1.025); the launches traced: 469 us -> 487 us
  Pallas kernels: 60.4 us -> 134 us
  waiting for transfers between devices: 240 us -> 195 us
  starting transfers between devices: 112 us -> 99.2 us
    pallas_call x2 -> x3, Pallas kernels: 55.6 us -> 129 us  [the longest x1 73.4 us: gather_params(): pl.pallas_call(lambda *refs: place_kernel(places, piece, *refs), out_shap...]
    all_to_all x5 -> x4, waiting for transfers between devices: 86.9 us -> 44.9 us  [exchange(): return lax.all_to_all(blocks, axes, split_axis=0, concat_axis=0, tiled=True)]
    ppermute x27, waiting for transfers between devices: 93.5 us -> 81.9 us  [along_z(): return lax.ppermute(values, 'z', [(i, (i + shift) % 4) for i in range(4)])]
    all_to_all x5 -> x4, starting transfers between devices: 31.2 us -> 21 us  [exchange(): return lax.all_to_all(blocks, axes, split_axis=0, concat_axis=0, tiled=True)]
    ppermute x20, waiting for transfers between devices: 59.8 us -> 67.7 us  [swap(): return lax.ppermute(values, axis, [(0, 1), (1, 0)])]
    ppermute x20, starting transfers between devices: 29.7 us -> 24.6 us  [swap(): return lax.ppermute(values, axis, [(0, 1), (1, 0)])]
  transfers between devices with their start and end apart: 52 -> 51, of which waited for: 24 -> 25; matrix products, arithmetic and copies ran while one was open for 9% -> 7% of each run, Pallas kernels for 5% -> 11%
where the time goes in v3:
time: 491 us; the launch traced here: 487 us
  waiting for transfers between devices  195 us (40%)
  Pallas kernels  134 us (27%)
  starting transfers between devices  99.2 us (20%)
  other arithmetic  22.8 us (5%)
  matrix products  20 us (4%)
  local copies, waits for them, and re-layouts  14.7 us (3%)
    ppermute x27, waiting for transfers between devices, along_z(): return lax.ppermute(values, 'z', [(i, (i + shift) % 4) for i in range(4)])  81.9 us
    pallas_call x1, Pallas kernels, gather_params(): pl.pallas_call(lambda *refs: place_kernel(places, piece, *refs), out_shap...  73.4 us
    ppermute x20, waiting for transfers between devices, swap(): return lax.ppermute(values, axis, [(0, 1), (1, 0)])  67.7 us
    pallas_call x2, Pallas kernels, experts(): pl.pallas_call(lambda *refs: expert_kernel(counts, pieces_out, tall, *ref...  55.9 us
    ppermute x27, starting transfers between devices, along_z(): return lax.ppermute(values, 'z', [(i, (i + shift) % 4) for i in range(4)])  53.7 us
    all_to_all x4, waiting for transfers between devices, exchange(): return lax.all_to_all(blocks, axes, split_axis=0, concat_axis=0, tiled=True)  44.9 us
    ppermute x20, starting transfers between devices, swap(): return lax.ppermute(values, axis, [(0, 1), (1, 0)])  24.6 us
    all_to_all x4, starting transfers between devices, exchange(): return lax.all_to_all(blocks, axes, split_axis=0, concat_axis=0, tiled=True)  21 us
  transfers between devices with their start and end apart: 51, of which 25 were waited for; matrix products, arithmetic and copies ran while one was open for 7% of the time, Pallas kernels for 11%

profile of v3, /device:TPU:0, one launch (start us, length us, event | category | flops | bytes accessed | tf_op | source)
XLA Modules:
  0.0 486.8 jit_solution(8644014296826658487)
XLA Ops:
  5.0 5.5 %all-to-all-start = ((bf16[16,8,3840]{2,1,0:T(8,128)(2,1)}), bf16[16,8,3840]{2,1,0:T(8,128)(2,1)S(1)}, u32[]{:S(2)}, u32[]{:S(2)}) async-start(bf16[16,8,3840]{2,1,0:T(8,128)(2,1)} %pad_maximum_fusion.4), calls=%async_computation | async-start | bytes 1966080 | tf_op jit(solution)/shard_map/all_to_all | solution.py:57
  10.6 3.0 collective-permute-start
  22.5 9.5 %collective-permute-done.refs_2_ = bf16[1152,128]{1,0:T(8,128)(2,1)S(1)} collective-permute-done((bf16[1152,128]{1,0:T(8,128)(2,1)S(1)}, bf16[1152,128]{1,0:T(8,128)(2,1)S(1)}, u32[]{:S(2)}, u32[]{:S(2)}) %collective-permute-start) | collective-permute-done | bytes 294944 | tf_op jit(solution)/shard_map/ppermute | solution.py:49
  42.9 3.6 collective-permute-done.5.refs_7_
  51.5 73.4 %shard_map.86 = bf16[8,1152,128]{2,1,0:T(8,128)(2,1)} custom-call(s32[2]{0:T(128)} %pad_add_fusion.refs_0_, bf16[1152,128]{1,0:T(8,128)(2,1)} %copy-done.20, bf16[1152,128]{1,0:T(8,128)(2,1)} %copy-done.22, bf16[576,128]{1,0:T(8,128)(2,1)} %copy-done.25, bf16[576,128]{1,0:T(8,128)(2,1)} %collective-permute-done.2.refs_4_, ...), custom_call_target="tpu_custom_call" | custom-call | tf_op jit(solution)/shard_map/pallas_call | solution.py:124
  133.5 8.4 %collective-permute-done.11.refs_7_ = bf16[80,3072]{1,0:T(8,128)(2,1)S(1)} collective-permute-done((bf16[80,3072]{1,0:T(8,128)(2,1)}, bf16[80,3072]{1,0:T(8,128)(2,1)S(1)}, u32[]{:S(2)}, u32[]{:S(2)}) %collective-permute-start.11) | collective-permute-done | bytes 491552 | tf_op jit(solution)/shard_map/ppermute | solution.py:53
  142.3 12.9 %collective-permute-done.17.refs_6_ = bf16[160,3072]{1,0:T(8,128)(2,1)} collective-permute-done((bf16[160,3072]{1,0:T(8,128)(2,1)}, bf16[160,3072]{1,0:T(8,128)(2,1)}, u32[]{:S(2)}, u32[]{:S(2)}) %collective-permute-start.17) | collective-permute-done | bytes 983072 | tf_op jit(solution)/shard_map/ppermute | solution.py:49
  170.6 4.8 all-to-all-start.1
  176.4 14.9 %collective-permute-start.19 = (bf16[160,3072]{1,0:T(8,128)(2,1)}, bf16[160,3072]{1,0:T(8,128)(2,1)}, u32[]{:S(2)}, u32[]{:S(2)}) collective-permute-start(bf16[160,3072]{1,0:T(8,128)(2,1)} %pad_maximum_fusion.7), channel_id=1, source_target_pairs={{0,96},{32,0},{64,32},{96,64},{1,97},{33,1},{65,33},{97,65},{2,98}... | collective-permute-start | bytes 2949128 | tf_op jit(solution)/shard_map/ppermute | solution.py:53
  199.0 8.8 %collective-permute-done.14.refs_7_ = bf16[80,3072]{1,0:T(8,128)(2,1)S(1)} collective-permute-done((bf16[80,3072]{1,0:T(8,128)(2,1)S(1)}, bf16[80,3072]{1,0:T(8,128)(2,1)S(1)}, u32[]{:S(2)}, u32[]{:S(2)}) %collective-permute-start.14) | collective-permute-done | bytes 491552 | tf_op jit(solution)/shard_map/ppermute | solution.py:49
  209.3 7.6 %collective-permute-done.16.refs_8_ = bf16[80,3072]{1,0:T(8,128)(2,1)S(1)} collective-permute-done((bf16[80,3072]{1,0:T(8,128)(2,1)S(1)}, bf16[80,3072]{1,0:T(8,128)(2,1)S(1)}, u32[]{:S(2)}, u32[]{:S(2)}) %collective-permute-start.16) | collective-permute-done | bytes 491552 | tf_op jit(solution)/shard_map/ppermute | solution.py:49
  216.9 17.0 %collective-permute-done.19.refs_10_ = bf16[160,3072]{1,0:T(8,128)(2,1)} collective-permute-done((bf16[160,3072]{1,0:T(8,128)(2,1)}, bf16[160,3072]{1,0:T(8,128)(2,1)}, u32[]{:S(2)}, u32[]{:S(2)}) %collective-permute-start.19) | collective-permute-done | bytes 983072 | tf_op jit(solution)/shard_map/ppermute | solution.py:53
  236.0 4.4 collective-permute-start.22
  241.1 10.6 %collective-permute-done.24.refs_4_ = bf16[80,3072]{1,0:T(8,128)(2,1)S(1)} collective-permute-done((bf16[80,3072]{1,0:T(8,128)(2,1)S(1)}, bf16[80,3072]{1,0:T(8,128)(2,1)S(1)}, u32[]{:S(2)}, u32[]{:S(2)}) %collective-permute-start.24) | collective-permute-done | bytes 491552 | tf_op jit(solution)/shard_map/ppermute | solution.py:53
  251.6 8.3 %collective-permute-done.22.refs_2_ = bf16[80,3072]{1,0:T(8,128)(2,1)S(1)} collective-permute-done((bf16[80,3072]{1,0:T(8,128)(2,1)S(1)}, bf16[80,3072]{1,0:T(8,128)(2,1)S(1)}, u32[]{:S(2)}, u32[]{:S(2)}) %collective-permute-start.22) | collective-permute-done | bytes 491552 | tf_op jit(solution)/shard_map/ppermute | solution.py:53
  267.1 23.5 %shard_map.87 = (bf16[160,3072]{1,0:T(8,128)(2,1)}, bf16[80,3072]{1,0:T(8,128)(2,1)S(1)}, bf16[80,3072]{1,0:T(8,128)(2,1)S(1)}, bf16[80,3072]{1,0:T(8,128)(2,1)S...) custom-call(bf16[160,3072]{1,0:T(8,128)(2,1)} %copy-done.13, bf16[160,3072]{1,0:T(8,128)(2,1)} %copy-done.24, ...), custom_call_target="tpu_custom_call" | custom-call | flops 11560550400 | bytes 22708224 | tf_op jit(solution)/shard_map/pallas_call | solution.py:274
  294.7 9.8 %collective-permute-done.29.refs_2_ = bf16[80,3072]{1,0:T(8,128)(2,1)S(1)} collective-permute-done((bf16[80,3072]{1,0:T(8,128)(2,1)S(1)}, bf16[80,3072]{1,0:T(8,128)(2,1)S(1)}, u32[]{:S(2)}, u32[]{:S(2)}) %collective-permute-start.29) | collective-permute-done | bytes 491552 | tf_op jit(solution)/shard_map/ppermute | solution.py:49
  311.8 32.3 %shard_map.88 = (bf16[80,3072]{1,0:T(8,128)(2,1)S(1)}, bf16[80,3072]{1,0:T(8,128)(2,1)S(1)}, bf16[80,3072]{1,0:T(8,128)(2,1)S(1)}, bf16[240,3072]{1,0:T(8,128)(2,1)}, bf16[240,3072]{1,0:T(8,128)(2,1)}) custom-call(bf16[80,3072]{1,0:T(8,128)(2,1)S(1)} %collective-permute-done.27.refs_0_, bf16[80,3072]{1,0:T(8,128)(2,1)S(1)} %collective-permute-done.28.refs_1_, ...), custom_call_target="tpu_custom_call" | custom-call | flops 14863564800 | bytes 25657344 | tf_op jit(solution)/shard_map/pallas_call | solution.py:274
  346.6 4.1 collective-permute-start.38
  350.8 11.0 %collective-permute-done.39 = bf16[80,3072]{1,0:T(8,128)(2,1)S(1)} collective-permute-done((bf16[80,3072]{1,0:T(8,128)(2,1)S(1)}, bf16[80,3072]{1,0:T(8,128)(2,1)S(1)}, u32[]{:S(2)}, u32[]{:S(2)}) %collective-permute-start.39) | collective-permute-done | bytes 491552 | tf_op jit(solution)/shard_map/ppermute | solution.py:53
  361.7 6.9 %collective-permute-done.38 = bf16[80,3072]{1,0:T(8,128)(2,1)S(1)} collective-permute-done((bf16[80,3072]{1,0:T(8,128)(2,1)S(1)}, bf16[80,3072]{1,0:T(8,128)(2,1)S(1)}, u32[]{:S(2)}, u32[]{:S(2)}) %collective-permute-start.38) | collective-permute-done | bytes 491552 | tf_op jit(solution)/shard_map/ppermute | solution.py:53
  370.7 10.5 %collective-permute-done.41 = bf16[240,3072]{1,0:T(8,128)(2,1)S(1)} collective-permute-done((bf16[240,3072]{1,0:T(8,128)(2,1)}, bf16[240,3072]{1,0:T(8,128)(2,1)S(1)}, u32[]{:S(2)}, u32[]{:S(2)}) %collective-permute-start.41) | collective-permute-done | bytes 1474592 | tf_op jit(solution)/shard_map/ppermute | solution.py:49
  382.5 3.4 collective-permute-start.43
  388.4 7.0 %collective-permute-done.44 = bf16[80,3072]{1,0:T(8,128)(2,1)S(1)} collective-permute-done((bf16[80,3072]{1,0:T(8,128)(2,1)S(1)}, bf16[80,3072]{1,0:T(8,128)(2,1)S(1)}, u32[]{:S(2)}, u32[]{:S(2)}) %collective-permute-start.44) | collective-permute-done | bytes 491552 | tf_op jit(solution)/shard_map/ppermute | solution.py:53
  395.4 5.1 %collective-permute-done.43 = bf16[80,3072]{1,0:T(8,128)(2,1)S(1)} collective-permute-done((bf16[80,3072]{1,0:T(8,128)(2,1)S(1)}, bf16[80,3072]{1,0:T(8,128)(2,1)S(1)}, u32[]{:S(2)}, u32[]{:S(2)}) %collective-permute-start.43) | collective-permute-done | bytes 491552 | tf_op jit(solution)/shard_map/ppermute | solution.py:53
  402.5 5.5 %all-to-all-start.2 = ((bf16[16,8,3840]{2,1,0:T(8,128)(2,1)}), bf16[16,8,3840]{2,1,0:T(8,128)(2,1)}, u32[]{:S(2)}, u32[]{:S(2)}) async-start(bf16[16,8,3840]{2,1,0:T(8,128)(2,1)} %pad_maximum_fusion.9), calls=%async_computation.2 | async-start | bytes 1966080 | tf_op jit(solution)/shard_map/all_to_all | solution.py:57
  408.1 15.8 %all-to-all-done.2 = bf16[16,8,3840]{2,1,0:T(8,128)(2,1)} async-done(((bf16[16,8,3840]{2,1,0:T(8,128)(2,1)}), bf16[16,8,3840]{2,1,0:T(8,128)(2,1)}, u32[]{:S(2)}, u32[]{:S(2)}) %all-to-all-start.2) | async-done | bytes 983072 | tf_op jit(solution)/shard_map/all_to_all | solution.py:57
  425.6 2.8 fusion.40
  441.7 4.6 shard_map.89
  446.3 5.3 %all-to-all-start.3 = ((bf16[64,144,128]{2,1,0:T(8,128)(2,1)}), bf16[64,144,128]{2,1,0:T(8,128)(2,1)S(1)}, u32[]{:S(2)}, u32[]{:S(2)}) async-start(bf16[64,144,128]{2,1,0:T(8,128)(2,1)} %shard_map.89), calls=%async_computation.3 | async-start | bytes 4718592 | tf_op jit(solution)/shard_map/all_to_all | solution.py:57
  451.6 3.3 fusion.83
  456.5 29.1 %all-to-all-done.3 = bf16[64,144,128]{2,1,0:T(8,128)(2,1)S(1)} async-done(((bf16[64,144,128]{2,1,0:T(8,128)(2,1)}), bf16[64,144,128]{2,1,0:T(8,128)(2,1)S(1)}, u32[]{:S(2)}, u32[]{:S(2)}) %all-to-all-start.3) | async-done | bytes 2359328 | tf_op jit(solution)/shard_map/all_to_all | solution.py:57
  (220 shorter events, 112.4 us)
Async XLA Ops:
  5.0 37.8 %all-to-all-start = ((bf16[16,8,3840]{2,1,0:T(8,128)(2,1)}), bf16[16,8,3840]{2,1,0:T(8,128)(2,1)S(1)}, u32[]{:S(2)}, u32[]{:S(2)}) async-start(bf16[16,8,3840]{2,1,0:T(8,128)(2,1)} %pad_maximum_fusion.4), calls=%async_computation | async-start | bytes 1966080 | tf_op jit(solution)/shard_map/all_to_all | solution.py:57
  10.6 21.4 %collective-permute-start = (bf16[1152,128]{1,0:T(8,128)(2,1)S(1)}, bf16[1152,128]{1,0:T(8,128)(2,1)S(1)}, u32[]{:S(2)}, u32[]{:S(2)}) collective-permute-start(bf16[1152,128]{1,0:T(8,128)(2,1)S(1)} %constant_dynamic-slice_fusion.2.refs_1_), channel_id=1, source_target_pairs={{0,16},{16,0},{1,17},{17,1},{2,18},{18,2},{3,19},{19,3},{4,20},{20... | collective-permute-start | bytes 884744 | tf_op jit(solution)/shard_map/ppermute | solution.py:49
  17.8 20.9 %collective-permute-start.3 = (bf16[576,128]{1,0:T(8,128)(2,1)S(1)}, bf16[576,128]{1,0:T(8,128)(2,1)}, u32[]{:S(2)}, u32[]{:S(2)}) collective-permute-start(bf16[576,128]{1,0:T(8,128)(2,1)S(1)} %get-tuple-element.74), channel_id=1, source_target_pairs={{0,64},{32,96},{64,0},{96,32},{1,65},{33,97},{65,1},{97,33},{2,66}... | collective-permute-start | bytes 442376 | tf_op jit(solution)/shard_map/ppermute | solution.py:53
  124.9 32.2 %collective-permute-start.10 = (bf16[8,1152,128]{2,1,0:T(8,128)(2,1)}, bf16[8,1152,128]{2,1,0:T(8,128)(2,1)}, u32[]{:S(2)}, u32[]{:S(2)}) collective-permute-start(bf16[8,1152,128]{2,1,0:T(8,128)(2,1)} %shard_map.86), channel_id=1, source_target_pairs={{0,1},{1,0},{2,3},{3,2},{4,5},{5,4},{6,7},{7,6},{8,9},{9,8},{10,11... | collective-permute-start | bytes 7077896 | tf_op jit(solution)/shard_map/ppermute | solution.py:49
  128.8 26.4 %collective-permute-start.17 = (bf16[160,3072]{1,0:T(8,128)(2,1)}, bf16[160,3072]{1,0:T(8,128)(2,1)}, u32[]{:S(2)}, u32[]{:S(2)}) collective-permute-start(bf16[160,3072]{1,0:T(8,128)(2,1)} %pad_maximum_fusion.3.refs_5_), channel_id=1, source_target_pairs={{0,16},{16,0},{1,17},{17,1},{2,18},{18,2},{3,19},{19,3},{4,20},{20... | collective-permute-start | bytes 2949128 | tf_op jit(solution)/shard_map/ppermute | solution.py:49
  130.4 46.0 %collective-permute-start.13 = (bf16[80,3072]{1,0:T(8,128)(2,1)}, bf16[80,3072]{1,0:T(8,128)(2,1)S(1)}, u32[]{:S(2)}, u32[]{:S(2)}) collective-permute-start(bf16[80,3072]{1,0:T(8,128)(2,1)} %slice.147), channel_id=1, source_target_pairs={{0,96},{32,0},{64,32},{96,64},{1,97},{33,1},{65,33},{97,65},{2,98}... | collective-permute-start | bytes 1474568 | tf_op jit(solution)/shard_map/ppermute | solution.py:53
  132.6 59.7 %collective-permute-start.15 = (bf16[80,3072]{1,0:T(8,128)(2,1)}, bf16[80,3072]{1,0:T(8,128)(2,1)S(1)}, u32[]{:S(2)}, u32[]{:S(2)}) collective-permute-start(bf16[80,3072]{1,0:T(8,128)(2,1)} %slice.147), channel_id=1, source_target_pairs={{0,64},{32,96},{64,0},{96,32},{1,65},{33,97},{65,1},{97,33},{2,66}... | collective-permute-start | bytes 1474568 | tf_op jit(solution)/shard_map/ppermute | solution.py:53
  141.9 52.2 %collective-permute-start.12 = (bf16[80,3072]{1,0:T(8,128)(2,1)S(1)}, bf16[80,3072]{1,0:T(8,128)(2,1)S(1)}, u32[]{:S(2)}, u32[]{:S(2)}) collective-permute-start(bf16[80,3072]{1,0:T(8,128)(2,1)S(1)} %collective-permute-done.11.refs_7_), channel_id=1, source_target_pairs={{0,16},{16,0},{1,17},{17,1},{2,18},{18,2},{3,19},{19,3},{4,20},{20... | collective-permute-start | bytes 1474568 | tf_op jit(solution)/shard_map/ppermute | solution.py:49
  170.6 25.3 %all-to-all-start.1 = ((bf16[16,8,3840]{2,1,0:T(8,128)(2,1)}), bf16[16,8,3840]{2,1,0:T(8,128)(2,1)}, u32[]{:S(2)}, u32[]{:S(2)}) async-start(bf16[16,8,3840]{2,1,0:T(8,128)(2,1)} %pad_maximum_fusion.5), calls=%async_computation.1 | async-start | bytes 1966080 | tf_op jit(solution)/shard_map/all_to_all | solution.py:57
  176.4 40.5 %collective-permute-start.18 = (bf16[160,3072]{1,0:T(8,128)(2,1)}, bf16[160,3072]{1,0:T(8,128)(2,1)}, u32[]{:S(2)}, u32[]{:S(2)}) collective-permute-start(bf16[160,3072]{1,0:T(8,128)(2,1)} %pad_maximum_fusion.7), channel_id=1, source_target_pairs={{0,32},{32,64},{64,96},{96,0},{1,33},{33,65},{65,97},{97,1},{2,34}... | collective-permute-start | bytes 2949128 | tf_op jit(solution)/shard_map/ppermute | solution.py:53
  176.4 57.6 %collective-permute-start.19 = (bf16[160,3072]{1,0:T(8,128)(2,1)}, bf16[160,3072]{1,0:T(8,128)(2,1)}, u32[]{:S(2)}, u32[]{:S(2)}) collective-permute-start(bf16[160,3072]{1,0:T(8,128)(2,1)} %pad_maximum_fusion.7), channel_id=1, source_target_pairs={{0,96},{32,0},{64,32},{96,64},{1,97},{33,1},{65,33},{97,65},{2,98}... | collective-permute-start | bytes 2949128 | tf_op jit(solution)/shard_map/ppermute | solution.py:53
  191.3 42.6 %collective-permute-start.20 = (bf16[160,3072]{1,0:T(8,128)(2,1)}, bf16[160,3072]{1,0:T(8,128)(2,1)}, u32[]{:S(2)}, u32[]{:S(2)}) collective-permute-start(bf16[160,3072]{1,0:T(8,128)(2,1)} %pad_maximum_fusion.7), channel_id=1, source_target_pairs={{0,64},{32,96},{64,0},{96,32},{1,65},{33,97},{65,1},{97,33},{2,66}... | collective-permute-start | bytes 2949128 | tf_op jit(solution)/shard_map/ppermute | solution.py:53
  194.1 22.8 %collective-permute-start.16 = (bf16[80,3072]{1,0:T(8,128)(2,1)S(1)}, bf16[80,3072]{1,0:T(8,128)(2,1)S(1)}, u32[]{:S(2)}, u32[]{:S(2)}) collective-permute-start(bf16[80,3072]{1,0:T(8,128)(2,1)S(1)} %collective-permute-done.15.refs_9_), channel_id=1, source_target_pairs={{0,16},{16,0},{1,17},{17,1},{2,18},{18,2},{3,19},{19,3},{4,20},{20... | collective-permute-start | bytes 1474568 | tf_op jit(solution)/shard_map/ppermute | solution.py:49
  207.9 32.6 %collective-permute-start.25 = (bf16[128,3072]{1,0:T(8,128)(2,1)}, bf16[128,3072]{1,0:T(8,128)(2,1)S(1)}, u32[]{:S(2)}, u32[]{:S(2)}) collective-permute-start(bf16[128,3072]{1,0:T(8,128)(2,1)} %fusion.13), channel_id=1, source_target_pairs={{0,1},{1,0},{2,3},{3,2},{4,5},{5,4},{6,7},{7,6},{8,9},{9,8},{10,11... | collective-permute-start | bytes 2359304 | tf_op jit(solution)/shard_map/ppermute | solution.py:49
  233.9 29.5 %collective-permute-start.21 = (bf16[160,3072]{1,0:T(8,128)(2,1)S(1)}, bf16[160,3072]{1,0:T(8,128)(2,1)S(1)}, u32[]{:S(2)}, u32[]{:S(2)}) collective-permute-start(bf16[160,3072]{1,0:T(8,128)(2,1)S(1)} %pad_maximum_fusion.6.refs_0_), channel_id=1, source_target_pairs={{0,16},{16,0},{1,17},{17,1},{2,18},{18,2},{3,19},{19,3},{4,20},{20... | collective-permute-start | bytes 2949128 | tf_op jit(solution)/shard_map/ppermute | solution.py:49
  236.0 23.9 %collective-permute-start.22 = (bf16[80,3072]{1,0:T(8,128)(2,1)S(1)}, bf16[80,3072]{1,0:T(8,128)(2,1)S(1)}, u32[]{:S(2)}, u32[]{:S(2)}) collective-permute-start(bf16[80,3072]{1,0:T(8,128)(2,1)S(1)} %get-tuple-element.72), channel_id=1, source_target_pairs={{0,32},{32,64},{64,96},{96,0},{1,33},{33,65},{65,97},{97,1},{2,34}... | collective-permute-start | bytes 1474568 | tf_op jit(solution)/shard_map/ppermute | solution.py:53
  240.5 21.1 %collective-permute-start.23 = (bf16[80,3072]{1,0:T(8,128)(2,1)S(1)}, bf16[80,3072]{1,0:T(8,128)(2,1)S(1)}, u32[]{:S(2)}, u32[]{:S(2)}) collective-permute-start(bf16[80,3072]{1,0:T(8,128)(2,1)S(1)} %get-tuple-element.72), channel_id=1, source_target_pairs={{0,96},{32,0},{64,32},{96,64},{1,97},{33,1},{65,33},{97,65},{2,98}... | collective-permute-start | bytes 1474568 | tf_op jit(solution)/shard_map/ppermute | solution.py:53
  259.9 30.7 %collective-permute-start.27 = (bf16[80,3072]{1,0:T(8,128)(2,1)S(1)}, bf16[80,3072]{1,0:T(8,128)(2,1)S(1)}, u32[]{:S(2)}, u32[]{:S(2)}) collective-permute-start(bf16[80,3072]{1,0:T(8,128)(2,1)S(1)} %collective-permute-done.22.refs_2_), channel_id=1, source_target_pairs={{0,16},{16,0},{1,17},{17,1},{2,18},{18,2},{3,19},{19,3},{4,20},{20... | collective-permute-start | bytes 1474568 | tf_op jit(solution)/shard_map/ppermute | solution.py:49
  261.6 31.0 %collective-permute-start.28 = (bf16[80,3072]{1,0:T(8,128)(2,1)S(1)}, bf16[80,3072]{1,0:T(8,128)(2,1)S(1)}, u32[]{:S(2)}, u32[]{:S(2)}) collective-permute-start(bf16[80,3072]{1,0:T(8,128)(2,1)S(1)} %collective-permute-done.23.refs_3_), channel_id=1, source_target_pairs={{0,16},{16,0},{1,17},{17,1},{2,18},{18,2},{3,19},{19,3},{4,20},{20... | collective-permute-start | bytes 1474568 | tf_op jit(solution)/shard_map/ppermute | solution.py:49
  263.6 42.2 %collective-permute-start.30 = (bf16[160,3072]{1,0:T(8,128)(2,1)S(1)}, bf16[160,3072]{1,0:T(8,128)(2,1)S(1)}, u32[]{:S(2)}, u32[]{:S(2)}) collective-permute-start(bf16[160,3072]{1,0:T(8,128)(2,1)S(1)} %pad_maximum_fusion.8), channel_id=1, source_target_pairs={{0,32},{32,64},{64,96},{96,0},{1,33},{33,65},{65,97},{97,1},{2,34}... | collective-permute-start | bytes 2949128 | tf_op jit(solution)/shard_map/ppermute | solution.py:53
  264.1 45.0 %collective-permute-start.31 = (bf16[160,3072]{1,0:T(8,128)(2,1)S(1)}, bf16[160,3072]{1,0:T(8,128)(2,1)S(1)}, u32[]{:S(2)}, u32[]{:S(2)}) collective-permute-start(bf16[160,3072]{1,0:T(8,128)(2,1)S(1)} %pad_maximum_fusion.8), channel_id=1, source_target_pairs={{0,96},{32,0},{64,32},{96,64},{1,97},{33,1},{65,33},{97,65},{2,98}... | collective-permute-start | bytes 2949128 | tf_op jit(solution)/shard_map/ppermute | solution.py:53
  266.9 43.9 %collective-permute-start.32 = (bf16[160,3072]{1,0:T(8,128)(2,1)S(1)}, bf16[160,3072]{1,0:T(8,128)(2,1)S(1)}, u32[]{:S(2)}, u32[]{:S(2)}) collective-permute-start(bf16[160,3072]{1,0:T(8,128)(2,1)S(1)} %pad_maximum_fusion.8), channel_id=1, source_target_pairs={{0,64},{32,96},{64,0},{96,32},{1,65},{33,97},{65,1},{97,33},{2,66}... | collective-permute-start | bytes 2949128 | tf_op jit(solution)/shard_map/ppermute | solution.py:53
  292.6 51.5 %collective-permute-start.33 = (bf16[80,3072]{1,0:T(8,128)(2,1)S(1)}, bf16[80,3072]{1,0:T(8,128)(2,1)S(1)}, u32[]{:S(2)}, u32[]{:S(2)}) collective-permute-start(bf16[80,3072]{1,0:T(8,128)(2,1)S(1)} %get-tuple-element.43), channel_id=1, source_target_pairs={{0,96},{32,0},{64,32},{96,64},{1,97},{33,1},{65,33},{97,65},{2,98}... | collective-permute-start | bytes 1474568 | tf_op jit(solution)/shard_map/ppermute | solution.py:53
  304.6 39.5 %collective-permute-start.34 = (bf16[80,3072]{1,0:T(8,128)(2,1)S(1)}, bf16[80,3072]{1,0:T(8,128)(2,1)S(1)}, u32[]{:S(2)}, u32[]{:S(2)}) collective-permute-start(bf16[80,3072]{1,0:T(8,128)(2,1)S(1)} %get-tuple-element.44), channel_id=1, source_target_pairs={{0,32},{32,64},{64,96},{96,0},{1,33},{33,65},{65,97},{97,1},{2,34}... | collective-permute-start | bytes 1474568 | tf_op jit(solution)/shard_map/ppermute | solution.py:53
  305.7 38.4 %collective-permute-start.35 = (bf16[80,3072]{1,0:T(8,128)(2,1)S(1)}, bf16[80,3072]{1,0:T(8,128)(2,1)S(1)}, u32[]{:S(2)}, u32[]{:S(2)}) collective-permute-start(bf16[80,3072]{1,0:T(8,128)(2,1)S(1)} %get-tuple-element.45), channel_id=1, source_target_pairs={{0,64},{32,96},{64,0},{96,32},{1,65},{33,97},{65,1},{97,33},{2,66}... | collective-permute-start | bytes 1474568 | tf_op jit(solution)/shard_map/ppermute | solution.py:53
  309.1 35.1 %collective-permute-start.36 = (bf16[80,3072]{1,0:T(8,128)(2,1)S(1)}, bf16[80,3072]{1,0:T(8,128)(2,1)S(1)}, u32[]{:S(2)}, u32[]{:S(2)}) collective-permute-start(bf16[80,3072]{1,0:T(8,128)(2,1)S(1)} %get-tuple-element.46), channel_id=1, source_target_pairs={{0,16},{16,0},{1,17},{17,1},{2,18},{18,2},{3,19},{19,3},{4,20},{20... | collective-permute-start | bytes 1474568 | tf_op jit(solution)/shard_map/ppermute | solution.py:49
  344.2 37.0 %collective-permute-start.41 = (bf16[240,3072]{1,0:T(8,128)(2,1)}, bf16[240,3072]{1,0:T(8,128)(2,1)S(1)}, u32[]{:S(2)}, u32[]{:S(2)}) collective-permute-start(bf16[240,3072]{1,0:T(8,128)(2,1)} %get-tuple-element.55), channel_id=1, source_target_pairs={{0,16},{16,0},{1,17},{17,1},{2,18},{18,2},{3,19},{19,3},{4,20},{20... | collective-permute-start | bytes 4423688 | tf_op jit(solution)/shard_map/ppermute | solution.py:49
  346.6 22.0 %collective-permute-start.38 = (bf16[80,3072]{1,0:T(8,128)(2,1)S(1)}, bf16[80,3072]{1,0:T(8,128)(2,1)S(1)}, u32[]{:S(2)}, u32[]{:S(2)}) collective-permute-start(bf16[80,3072]{1,0:T(8,128)(2,1)S(1)} %get-tuple-element.48), channel_id=1, source_target_pairs={{0,32},{32,64},{64,96},{96,0},{1,33},{33,65},{65,97},{97,1},{2,34}... | collective-permute-start | bytes 1474568 | tf_op jit(solution)/shard_map/ppermute | solution.py:53
  368.9 19.5 %collective-permute-start.40 = (bf16[80,3072]{1,0:T(8,128)(2,1)S(1)}, bf16[80,3072]{1,0:T(8,128)(2,1)S(1)}, u32[]{:S(2)}, u32[]{:S(2)}) collective-permute-start(bf16[80,3072]{1,0:T(8,128)(2,1)S(1)} %add_convert_fusion.3), channel_id=1, source_target_pairs={{0,16},{16,0},{1,17},{17,1},{2,18},{18,2},{3,19},{19,3},{4,20},{20... | collective-permute-start | bytes 1474568 | tf_op jit(solution)/shard_map/ppermute | solution.py:49
  382.5 18.0 %collective-permute-start.43 = (bf16[80,3072]{1,0:T(8,128)(2,1)S(1)}, bf16[80,3072]{1,0:T(8,128)(2,1)S(1)}, u32[]{:S(2)}, u32[]{:S(2)}) collective-permute-start(bf16[80,3072]{1,0:T(8,128)(2,1)S(1)} %get-tuple-element.68), channel_id=1, source_target_pairs={{0,32},{32,64},{64,96},{96,0},{1,33},{33,65},{65,97},{97,1},{2,34}... | collective-permute-start | bytes 1474568 | tf_op jit(solution)/shard_map/ppermute | solution.py:53
  402.5 21.3 %all-to-all-start.2 = ((bf16[16,8,3840]{2,1,0:T(8,128)(2,1)}), bf16[16,8,3840]{2,1,0:T(8,128)(2,1)}, u32[]{:S(2)}, u32[]{:S(2)}) async-start(bf16[16,8,3840]{2,1,0:T(8,128)(2,1)} %pad_maximum_fusion.9), calls=%async_computation.2 | async-start | bytes 1966080 | tf_op jit(solution)/shard_map/all_to_all | solution.py:57
  446.3 39.3 %all-to-all-start.3 = ((bf16[64,144,128]{2,1,0:T(8,128)(2,1)}), bf16[64,144,128]{2,1,0:T(8,128)(2,1)S(1)}, u32[]{:S(2)}, u32[]{:S(2)}) async-start(bf16[64,144,128]{2,1,0:T(8,128)(2,1)} %shard_map.89), calls=%async_computation.3 | async-start | bytes 4718592 | tf_op jit(solution)/shard_map/all_to_all | solution.py:57
  (52 other events, 819.6 us)
